TPU v7x, 256 devices: a whole 4x4x8 slice. The times are simulated.
256 devices in a mesh: tel: 8 (over y, core), leaf: 32 (over z, x).
Axes of the slice: x: 4, y: 4, z: 8, core: 2. Of those that a mesh axis runs over, the one named last changes fastest.
Arguments:
- values: bfloat16 [32, 256, 8, 256], P('leaf', 'tel'), may hold values from -6 to 6
- basis: bfloat16 [32, 256, 64, 256], P('leaf', 'tel'), may hold values from -0.375 to 0.375
- transfer_b: bfloat16 [32, 32, 64, 512], P('leaf', 'tel'), may hold values from -0.5 to 0.5
- transfer_c: bfloat16 [32, 4, 64, 512], P('leaf'), may hold values from -0.5 to 0.5
- coupling_a: bfloat16 [32, 256, 24, 4096], P('leaf', 'tel'), may hold values from -0.21875 to 0.21875
- lists_a: int32 [32, 256, 24], P('leaf', 'tel'), may hold values from 0 to 8191, as said below
- mask_a: int32 [32, 256, 24], P('leaf', 'tel'), may hold values from 0 to 1, as said below
- coupling_b: bfloat16 [32, 32, 24, 4096], P('leaf', 'tel'), may hold values from -0.21875 to 0.21875
- lists_b: int32 [32, 32, 24], P('leaf', 'tel'), may hold values from 0 to 1023, as said below
- mask_b: int32 [32, 32, 24], P('leaf', 'tel'), may hold values from 0 to 1, as said below
- coupling_c: bfloat16 [32, 4, 24, 4096], P('leaf', None, 'tel'), may hold values from -0.21875 to 0.21875
- lists_c: int32 [32, 4, 24], P('leaf', None, 'tel'), may hold values from 0 to 127, as said below
- mask_c: int32 [32, 4, 24], P('leaf', None, 'tel'), may hold values from 0 to 1, as said below
Outputs:
- field: bfloat16 [32, 256, 8, 256], P('leaf', 'tel')
Inputs may be any that keep to these rules, and one draw needn't show every extreme that they name: `lists_a`: the partner of a leaf in group g is a leaf of group g - 1, g or g + 1; both ends of the range occur. `lists_b`: the partner of a parent box in group g is a parent box of group g - 1, g or g + 1; both ends of the range occur. `lists_c`: partners of grandparent boxes may be any grandparent box; both ends of the range occur. `mask_a`: every list row has between a quarter of its entries and all of them valid, in any positions. `mask_b`: as for mask_a. `mask_c`: as for mask_a, counted over the whole row of 24 entries.
All inputs are finite; a program needn't handle non-finite values.
Results may differ from a plain program's by a relative error of at most 0.015.
Values may be sent and summed in bfloat16 or wider, within the bound.
A program may use at most 128 MiB of HBM per device.

v0:
```python
import jax
import jax.numpy as jnp
from jax import lax
from jax.sharding import PartitionSpec as P


def with_halo(block, sides, width):
    for axis, dim in sides:
        count = lax.axis_size(axis)
        forward = [(i, i + 1) for i in range(count - 1)]
        backward = [(target, source) for source, target in forward]
        low = lax.ppermute(
            lax.slice_in_dim(block, block.shape[dim] - width, None, axis=dim), axis, forward
        )
        high = lax.ppermute(lax.slice_in_dim(block, 0, width, axis=dim), axis, backward)
        block = jnp.concatenate([low, block, high], axis=dim)
    return block


def couple(coupling, lists, mask, source, offset):
    count, slots = lists.shape
    rank_dim = source.shape[1]
    picked = jnp.take(source, lists - offset, axis=0)
    picked = picked * mask.astype(jnp.bfloat16)[:, :, None, None]
    blocks = coupling.reshape(count, slots, rank_dim, rank_dim)
    return jnp.einsum("npkm,npmr->nkr", blocks, picked, preferred_element_type=jnp.float32)


def on_device(
    values,
    basis,
    transfer_b,
    transfer_c,
    coupling_a,
    lists_a,
    mask_a,
    coupling_b,
    lists_b,
    mask_b,
    coupling_c,
    lists_c,
    mask_c,
):
    group = lax.axis_index("leaf")
    member = lax.axis_index("tel")
    tel_count = lax.axis_size("tel")
    own_leaves = values.shape[1]
    rhs_dim = values.shape[2]
    rank_dim = basis.shape[2]
    own_parents = transfer_b.shape[1]
    group_len = own_leaves * tel_count
    group_parents = own_parents * tel_count
    group_grands = transfer_c.shape[1]
    q_leaf = jnp.einsum(
        "nkp,nrp->nkr", basis[0], values[0], preferred_element_type=jnp.float32
    ).astype(jnp.bfloat16)
    q_parent = jnp.einsum(
        "bkm,bmr->bkr",
        transfer_b[0],
        q_leaf.reshape(own_parents, 8 * rank_dim, rhs_dim),
        preferred_element_type=jnp.float32,
    ).astype(jnp.bfloat16)
    group_q = lax.all_gather(q_leaf, "tel", axis=0, tiled=True)
    window_leaf = with_halo(group_q, (("leaf", 0),), group_len)
    near_leaf = couple(coupling_a[0], lists_a[0], mask_a[0], window_leaf, (group - 1) * group_len)
    group_b = lax.all_gather(q_parent, "tel", axis=0, tiled=True)
    window_parent = with_halo(group_b, (("leaf", 0),), group_parents)
    parent_offset = (group - 1) * group_parents
    q_grand = jnp.einsum(
        "ckm,cmr->ckr",
        transfer_c[0],
        group_b.reshape(group_grands, 8 * rank_dim, rhs_dim),
        preferred_element_type=jnp.float32,
    ).astype(jnp.bfloat16)
    top_grand = lax.all_gather(q_grand, "leaf", axis=0, tiled=True)
    share = couple(coupling_c[0], lists_c[0], mask_c[0], top_grand, 0)
    y_grand = lax.psum(share, "tel").astype(jnp.bfloat16)
    near_parent = couple(coupling_b[0], lists_b[0], mask_b[0], window_parent, parent_offset)
    down_grand = jnp.einsum(
        "ckm,ckr->cmr", transfer_c[0], y_grand, preferred_element_type=jnp.float32
    ).reshape(group_parents, rank_dim, rhs_dim)
    own_down = lax.dynamic_slice_in_dim(down_grand, member * own_parents, own_parents, 0)
    y_parent = (near_parent + own_down).astype(jnp.bfloat16)
    down_parent = jnp.einsum(
        "bkm,bkr->bmr", transfer_b[0], y_parent, preferred_element_type=jnp.float32
    ).reshape(own_leaves, rank_dim, rhs_dim)
    y_leaf = (near_leaf + down_parent).astype(jnp.bfloat16)
    field = jnp.einsum("nkp,nkr->nrp", basis[0], y_leaf, preferred_element_type=jnp.float32).astype(
        jnp.bfloat16
    )
    return field[None]


def solution(mesh):
    in_specs = (
        P("leaf", "tel", None, None),
        P("leaf", "tel", None, None),
        P("leaf", "tel", None, None),
        P("leaf", None, None, None),
        P("leaf", "tel", None, None),
        P("leaf", "tel", None),
        P("leaf", "tel", None),
        P("leaf", "tel", None, None),
        P("leaf", "tel", None),
        P("leaf", "tel", None),
        P("leaf", None, "tel", None),
        P("leaf", None, "tel"),
        P("leaf", None, "tel"),
    )
    out_specs = P("leaf", "tel", None, None)
    return jax.shard_map(
        on_device, mesh=mesh, in_specs=in_specs, out_specs=out_specs, check_vma=False
    )
```

profile of v0, /device:TPU:102, one launch (start us, length us, event | category | flops | bytes accessed | tf_op | source)
XLA Modules:
  0.0 166.8 jit_solution(14169078401927497744)
XLA Ops:
  0.1 1.2 copy-done
  1.2 1.3 convolution_convert_fusion.1
  2.6 1.1 fusion.16
  3.7 14.3 %all_gather.10 = bf16[32,64,8]{1,2,0:T(8,128)(2,1)} all-gather(bf16[4,64,8]{1,2,0:T(8,128)(2,1)S(1)} %fusion.16), channel_id=1, replica_groups=mesh['tel'=8,'leaf'=32] {'tel'}, dimensions={0}, use_global_device_ids=true | all-gather | bytes 36864 | tf_op jit(solution)/shard_map/all_gather | solution.py:66
  18.1 2.7 %collective-permute-start.3 = (bf16[32,64,8]{1,2,0:T(8,128)(2,1)}, bf16[32,64,8]{1,2,0:T(8,128)(2,1)}, u32[]{:S(2)}, u32[]{:S(2)}) collective-permute-start(bf16[32,64,8]{1,2,0:T(8,128)(2,1)} %all_gather.10), channel_id=1, source_target_pairs={{1,0},{2,1},{3,2},{4,3},{5,4},{6,5},{7,6},{8,7},{9,8},{10,9},{11,1... | collective-permute-start | bytes 98312 | tf_op jit(solution)/shard_map/ppermute | solution.py:15
  20.8 6.4 %collective-permute-start.2 = (bf16[32,64,8]{1,2,0:T(8,128)(2,1)}, bf16[32,64,8]{1,2,0:T(8,128)(2,1)}, u32[]{:S(2)}, u32[]{:S(2)}) collective-permute-start(bf16[32,64,8]{1,2,0:T(8,128)(2,1)} %all_gather.10), channel_id=1, source_target_pairs={{0,1},{1,2},{2,3},{3,4},{4,5},{5,6},{6,7},{7,8},{8,9},{9,10},{10,1... | collective-permute-start | bytes 98312 | tf_op jit(solution)/shard_map/ppermute | solution.py:12
  27.2 13.1 %all_gather.9 = bf16[256,64,8]{1,2,0:T(8,128)(2,1)S(1)} all-gather(bf16[32,64,8]{1,2,0:T(8,128)(2,1)S(1)} %convolution_convert_fusion.1), channel_id=1, replica_groups=mesh['tel'=8,'leaf'=32] {'tel'}, dimensions={0}, use_global_device_ids=true | all-gather | bytes 294912 | tf_op jit(solution)/shard_map/all_gather | solution.py:63
  40.3 1.9 %collective-permute-start.1 = (bf16[256,64,8]{1,2,0:T(8,128)(2,1)S(1)}, bf16[256,64,8]{1,2,0:T(8,128)(2,1)}, u32[]{:S(2)}, u32[]{:S(2)}) collective-permute-start(bf16[256,64,8]{1,2,0:T(8,128)(2,1)S(1)} %all_gather.9), channel_id=1, source_target_pairs={{1,0},{2,1},{3,2},{4,3},{5,4},{6,5},{7,6},{8,7},{9,8},{10,9},{11,1... | collective-permute-start | bytes 786440 | tf_op jit(solution)/shard_map/ppermute | solution.py:15
  42.3 7.2 %collective-permute-start = (bf16[256,64,8]{1,2,0:T(8,128)(2,1)S(1)}, bf16[256,64,8]{1,2,0:T(8,128)(2,1)}, u32[]{:S(2)}, u32[]{:S(2)}) collective-permute-start(bf16[256,64,8]{1,2,0:T(8,128)(2,1)S(1)} %all_gather.9), channel_id=1, source_target_pairs={{0,1},{1,2},{2,3},{3,4},{4,5},{5,6},{6,7},{7,8},{8,9},{9,10},{10,1... | collective-permute-start | bytes 786440 | tf_op jit(solution)/shard_map/ppermute | solution.py:12
  49.5 0.6 compare_and_fusion.2
  50.3 0.9 copy.39
  51.1 0.6 convert_bitcast_fusion.1
  52.8 51.6 %all_gather.11 = bf16[128,64,8]{1,2,0:T(8,128)(2,1)S(1)} all-gather(bf16[4,64,8]{1,2,0:T(8,128)(2,1)S(1)} %fusion.17), channel_id=1, replica_groups=mesh['tel'=8,'leaf'=32] {'leaf'}, dimensions={0}, use_global_device_ids=true | all-gather | bytes 135168 | tf_op jit(solution)/shard_map/all_gather | solution.py:75
  105.2 23.6 %psum.7 = bf16[4,64,8]{1,2,0:T(8,128)(2,1)S(1)} all-reduce(f32[4,64,8]{1,2,0:T(8,128)S(1)} %convolution_bitcast_fusion.2), channel_id=1, replica_groups=mesh['tel'=8,'leaf'=32] {'tel'}, use_global_device_ids=true, to_apply=%region_0.1 | all-reduce | flops 2048 | bytes 12288 | tf_op jit(solution)/shard_map/psum | solution.py:77
  129.1 0.6 constant_dynamic-slice_fusion
  129.7 0.7 copy.33
  130.4 2.5 %reshape_squeeze.10 = bf16[4,24,64,64]{3,2,1,0:T(8,128)(2,1)S(1)} reshape(bf16[1,4,24,4096]{3,2,1,0:T(8,128)(2,1)} %param.20) | data formatting | bytes 1572864 | tf_op jit(solution)/shard_map/reshape;squeeze | solution.py:25
  133.0 17.9 %reshape_squeeze.9 = bf16[32,24,64,64]{3,2,1,0:T(8,128)(2,1)} reshape(bf16[1,32,24,4096]{3,2,1,0:T(8,128)(2,1)} %param.17) | data formatting | bytes 12582912 | tf_op jit(solution)/shard_map/reshape;squeeze | solution.py:25
  150.9 1.0 pad_maximum_fusion.1
  151.9 0.7 gather_fusion.1
  152.6 1.7 convolution_bitcast_fusion
  154.4 1.5 pad_maximum_fusion
  156.0 3.2 %gather_fusion = bf16[768,64,8]{1,2,0:T(8,128)(2,1)} fusion(bf16[768,64,8]{1,2,0:T(8,128)(2,1)S(1)} %pad_maximum_fusion, s32[1024]{0:T(1024)S(1)} %pad_clamp_fusion.2), kind=kCustom, calls=%fused_computation | custom fusion | bytes 1575936 | tf_op jit(solution)/shard_map/jit(_take)/gather | solution.py:23
  159.1 7.6 %fusion.4 = bf16[1,32,8,256]{3,2,1,0:T(8,128)(2,1)} fusion(bf16[1,32,64,256]{3,2,1,0:T(8,128)(2,1)S(1)} %copy-done, bf16[32,24,64,64]{3,2,1,0:T(8,128)(2,1)} %reshape_squeeze.9, bf16[32,24,64,8]{2,3,1,0:T(8,128)(2,1)} %bitcast.104, pred[32,24]{1,0:T(8,128)(4,1)S(1)} %copy-done.7, bf16[32,24]{1,0:T(8,128)(2,1)S(1)} %copy.35, f32[32,64,8]{1,0,2:T(8,128)S(1)} %reshape.125), kind=kOutput, calls=%fused_computation.9 | convolution fusion | flops 59604992 | bytes 8325376 | tf_op jit(solution)/shard_map/nkp,nkr->nrp/dot_general | solution.py:88
  (53 shorter events, 2.7 us)
Async XLA Ops:
  0.0 1.2 copy-start
  0.0 49.5 %copy-start.5 = (s32[1,4,24]{2,1,0:T(4,128)S(1)}, s32[1,4,24]{2,1,0:T(4,128)}, u32[]{:S(2)}) copy-start(s32[1,4,24]{2,1,0:T(4,128)} %param.21) | copy-start | bytes 1156
  0.0 50.1 %copy-start.6 = (s32[1,4,3]{1,0,2:T(1,128)S(1)}, s32[1,4,3]{1,0,2:T(1,128)}, u32[]{:S(2)}) copy-start(s32[1,4,3]{1,0,2:T(1,128)} %param.24) | copy-start | bytes 148
  0.0 50.2 %copy-start.3 = (s32[1,32,24]{1,2,0:T(8,128)S(1)}, s32[1,32,24]{1,2,0:T(8,128)}, u32[]{:S(2)}) copy-start(s32[1,32,24]{1,2,0:T(8,128)} %param.18) | copy-start | bytes 9220
  0.0 51.1 %copy-start.8 = (s32[1,4,24]{2,1,0:T(4,128)S(1)}, s32[1,4,24]{2,1,0:T(4,128)}, u32[]{:S(2)}) copy-start(s32[1,4,24]{2,1,0:T(4,128)} %param.22) | copy-start | bytes 1156
  0.0 51.8 %copy-start.9 = (s32[1,4,3]{1,0,2:T(1,128)S(1)}, s32[1,4,3]{1,0,2:T(1,128)}, u32[]{:S(2)}) copy-start(s32[1,4,3]{1,0,2:T(1,128)} %param.25) | copy-start | bytes 148
  0.0 52.1 %copy-start.4 = (s32[1,32,24]{1,2,0:T(8,128)S(1)}, s32[1,32,24]{1,2,0:T(8,128)}, u32[]{:S(2)}) copy-start(s32[1,32,24]{1,2,0:T(8,128)} %param.19) | copy-start | bytes 9220
  0.1 52.4 %copy-start.2 = (bf16[1,4,3,4096]{3,1,2,0:T(4,128)(2,1)S(1)}, bf16[1,4,3,4096]{3,1,2,0:T(4,128)(2,1)}, u32[]{:S(2)}) copy-start(bf16[1,4,3,4096]{3,1,2,0:T(4,128)(2,1)} %param.23) | copy-start | bytes 294916
  0.1 52.6 %copy-start.1 = (bf16[1,4,64,512]{3,2,1,0:T(8,128)(2,1)S(1)}, bf16[1,4,64,512]{3,2,1,0:T(8,128)(2,1)}, u32[]{:S(2)}) copy-start(bf16[1,4,64,512]{3,2,1,0:T(8,128)(2,1)} %param.16) | copy-start | bytes 786436
  18.1 132.9 %collective-permute-start.3 = (bf16[32,64,8]{1,2,0:T(8,128)(2,1)}, bf16[32,64,8]{1,2,0:T(8,128)(2,1)}, u32[]{:S(2)}, u32[]{:S(2)}) collective-permute-start(bf16[32,64,8]{1,2,0:T(8,128)(2,1)} %all_gather.10), channel_id=1, source_target_pairs={{1,0},{2,1},{3,2},{4,3},{5,4},{6,5},{7,6},{8,7},{9,8},{10,9},{11,1... | collective-permute-start | bytes 98312 | tf_op jit(solution)/shard_map/ppermute | solution.py:15
  20.8 130.1 %collective-permute-start.2 = (bf16[32,64,8]{1,2,0:T(8,128)(2,1)}, bf16[32,64,8]{1,2,0:T(8,128)(2,1)}, u32[]{:S(2)}, u32[]{:S(2)}) collective-permute-start(bf16[32,64,8]{1,2,0:T(8,128)(2,1)} %all_gather.10), channel_id=1, source_target_pairs={{0,1},{1,2},{2,3},{3,4},{4,5},{5,6},{6,7},{7,8},{8,9},{9,10},{10,1... | collective-permute-start | bytes 98312 | tf_op jit(solution)/shard_map/ppermute | solution.py:12
  40.3 114.1 %collective-permute-start.1 = (bf16[256,64,8]{1,2,0:T(8,128)(2,1)S(1)}, bf16[256,64,8]{1,2,0:T(8,128)(2,1)}, u32[]{:S(2)}, u32[]{:S(2)}) collective-permute-start(bf16[256,64,8]{1,2,0:T(8,128)(2,1)S(1)} %all_gather.9), channel_id=1, source_target_pairs={{1,0},{2,1},{3,2},{4,3},{5,4},{6,5},{7,6},{8,7},{9,8},{10,9},{11,1... | collective-permute-start | bytes 786440 | tf_op jit(solution)/shard_map/ppermute | solution.py:15
  42.3 112.1 %collective-permute-start = (bf16[256,64,8]{1,2,0:T(8,128)(2,1)S(1)}, bf16[256,64,8]{1,2,0:T(8,128)(2,1)}, u32[]{:S(2)}, u32[]{:S(2)}) collective-permute-start(bf16[256,64,8]{1,2,0:T(8,128)(2,1)S(1)} %all_gather.9), channel_id=1, source_target_pairs={{0,1},{1,2},{2,3},{3,4},{4,5},{5,6},{6,7},{7,8},{8,9},{9,10},{10,1... | collective-permute-start | bytes 786440 | tf_op jit(solution)/shard_map/ppermute | solution.py:12
  155.9 3.2 %copy-start.7 = (pred[32,24]{1,0:T(8,128)(4,1)S(1)}, pred[32,24]{1,0:T(8,128)(4,1)}, u32[]{:S(2)}) copy-start(pred[32,24]{1,0:T(8,128)(4,1)} %copy.33) | copy-start | bytes 2308
where the time goes:
time: 169 us; the launch traced here: 167 us
  blocking collectives  103 us (61%)
  local copies, waits for them, and re-layouts  29.7 us (18%)
  starting transfers between devices  18.3 us (11%)
  matrix products  12.2 us (7%)
  other arithmetic  3.75 us (2%)
    all_gather x1, blocking collectives, on_device(): top_grand = lax.all_gather(q_grand, 'leaf', axis=0, tiled=True)  51.6 us
    psum x1, blocking collectives, on_device(): y_grand = lax.psum(share, 'tel').astype(jnp.bfloat16)  23.6 us
    another operation x3, local copies, waits for them, and re-layouts, couple(): blocks = coupling.reshape(count, slots, rank_dim, rank_dim)  20.7 us
    all_gather x1, blocking collectives, on_device(): group_b = lax.all_gather(q_parent, 'tel', axis=0, tiled=True)  14.3 us
    ppermute x2, starting transfers between devices, with_halo(): lax.ppermute(lax.slice_in_dim(block, block.shape[dim] - width, None, axis...  13.7 us
    all_gather x1, blocking collectives, on_device(): group_q = lax.all_gather(q_leaf, 'tel', axis=0, tiled=True)  13.1 us
    dot_general x1, matrix products, on_device(): jnp.einsum('nkp,nkr->nrp', basis[0], y_leaf, preferred_element_type=jnp.f...  7.62 us
    ppermute x2, starting transfers between devices, with_halo(): lax.ppermute(lax.slice_in_dim(block, 0, width, axis=dim), axis, backward)  4.64 us
  transfers between devices with their start and end apart: 4, of which 0 were waited for; matrix products, arithmetic and copies ran while one was open for 18% of the time, Pallas kernels for 0%

commit v1 on v0

v1 whole, which is shorter than its diff:
```python
import functools

import jax
import jax.numpy as jnp
from jax import lax
from jax.experimental import pallas as pl
from jax.experimental.pallas import tpu as pltpu
from jax.sharding import PartitionSpec as P

BF = jnp.bfloat16
F32 = jnp.float32
MESH = pl.DeviceIdType.MESH


def nt(a, b):
    return lax.dot_general(a, b, (((1,), (1,)), ((), ())), preferred_element_type=F32)


def nn(a, b):
    return jnp.dot(a, b, preferred_element_type=F32)


def grid_index(shape, dim):
    return lax.broadcasted_iota(jnp.int32, shape, dim)


def flag(condition):
    return jnp.where(condition, 1.0, 0.0)


def column(rows, height, stride):
    sub, lane = grid_index((height, 128), 0), grid_index((height, 128), 1)
    total = jnp.zeros((height, 128), F32)
    for place, row in enumerate(rows):
        width = row.shape[1]
        wide = jnp.concatenate([row.astype(F32), jnp.zeros((1, 128 - width), F32)], axis=1)
        hit = (lane == sub - place * stride) & (lane < width)
        total = total + jnp.where(hit, jnp.broadcast_to(wide, (height, 128)), 0.0)
    return jnp.sum(total, axis=1, keepdims=True).astype(jnp.int32)


def kernel(
    groups,
    values,
    basis,
    transfer_b,
    transfer_c,
    coupling_a,
    coupling_b,
    coupling_c,
    lists_a,
    mask_a,
    lists_b,
    mask_b,
    lists_c,
    mask_c,
    field,
    v_values,
    v_basis,
    v_tb,
    v_tc,
    v_ca,
    v_cb,
    v_cc,
    leaf_window,
    parent_window,
    grand_window,
    share_out,
    share_in,
    pick_a,
    picked,
    near,
    load_sem,
    y_send,
    y_recv,
    x_send,
    x_recv,
    mate_send,
    mate_recv,
    b_send,
    b_recv,
    bx_send,
    bx_recv,
    c_send,
    c_recv,
    s_send,
    s_recv,
):
    g = lax.axis_index("leaf")
    t = lax.axis_index("tel")
    y, core = t // 2, t % 2
    up, down = lax.rem(g + 1, groups), lax.rem(g + groups - 1, groups)

    loads = [
        pltpu.make_async_copy(source, target, load_sem.at[place])
        for place, (source, target) in enumerate(
            (
                (values, v_values),
                (basis, v_basis),
                (transfer_b, v_tb),
                (transfer_c, v_tc),
                (coupling_c, v_cc),
                (coupling_b, v_cb),
                (coupling_a, v_ca),
            )
        )
    ]
    for load in loads:
        load.start()

    barrier = pltpu.get_barrier_semaphore()

    def greet_group(d, carry):
        pl.semaphore_signal(
            barrier, inc=1, device_id={"tel": lax.rem(t + d, 8), "leaf": g}, device_id_type=MESH
        )
        return carry

    def greet_plane(d, carry):
        pl.semaphore_signal(
            barrier, inc=1, device_id={"tel": t, "leaf": lax.rem(g + d, groups)}, device_id_type=MESH
        )
        return carry

    lax.fori_loop(1, 8, greet_group, 0)
    lax.fori_loop(1, groups, greet_plane, 0)

    sub, lane = grid_index((8, 128), 0), grid_index((8, 128), 1)
    left = lane < 64
    even_left = (sub % 2 == 0) & left
    odd_right = (sub % 2 == 1) & (lane >= 64)

    loads[0].wait()
    loads[1].wait()
    placed, stacked = [], []
    for s in range(8):
        product = nt(v_values[32 * s : 32 * s + 32, :], v_basis[256 * s : 256 * s + 256, :])
        for h in range(2):
            first = product[16 * h : 16 * h + 8, 128 * h : 128 * h + 128]
            second = product[16 * h + 8 : 16 * h + 16, 128 * h : 128 * h + 128]
            placed.append(
                jnp.where(even_left, first, jnp.where(odd_right, pltpu.roll(first, 64, 1), 0.0))
            )
            placed.append(
                jnp.where(even_left, pltpu.roll(second, 64, 1), jnp.where(odd_right, second, 0.0))
            )
            stacked.append(jnp.where(left, first, second))
    placed = jnp.concatenate(placed, axis=0).astype(BF)
    row, col = grid_index((128, 256), 0), grid_index((128, 256), 1)
    order = flag((row % 32 == col // 8) & (row // 32 == (col % 8) // 2)).astype(BF)
    own_slot = 8 + core * 4 + y
    leaf_window[own_slot] = nn(order, placed).astype(BF)

    loads[2].wait()
    lifted = []
    for b in range(4):
        children = jnp.concatenate(stacked[4 * b : 4 * b + 4], axis=1).astype(BF)
        lifted.append(nt(children, v_tb[64 * b : 64 * b + 64, :]))
    parent_window[8 + t] = jnp.concatenate(
        [jnp.concatenate(lifted[0:2], axis=1), jnp.concatenate(lifted[2:4], axis=1)], axis=0
    ).astype(BF)

    pl.semaphore_wait(barrier, 7 + groups - 1)

    def send(source, target, send_sem, recv_sem, tel, leaf):
        copy = pltpu.make_async_remote_copy(
            src_ref=source,
            dst_ref=target,
            send_sem=send_sem,
            recv_sem=recv_sem,
            device_id={"tel": tel, "leaf": leaf},
            device_id_type=MESH,
        )
        copy.start()
        return copy

    sent = []
    for d in range(1, 8):
        block = parent_window.at[8 + t]
        sent.append(send(block, block, b_send.at[d - 1], b_recv.at[0], lax.rem(t + d, 8), g))

    mate = t + 1 - 2 * core

    def spread(slot, place):
        block = leaf_window.at[slot]
        sent.append(
            send(block, leaf_window.at[slot - 8], x_send.at[place], x_recv.at[place], t, up)
        )
        sent.append(
            send(block, leaf_window.at[slot + 8], x_send.at[4 + place], x_recv.at[4 + place], t, down)
        )
        sent.append(send(block, block, mate_send.at[place], mate_recv.at[place], mate, g))

    own = leaf_window.at[own_slot]
    for d in range(1, 4):
        sent.append(
            send(own, own, y_send.at[d - 1], y_recv.at[d - 1], lax.rem(y + d, 4) * 2 + core, g)
        )
    spread(own_slot, 0)

    local = lists_a[...] - (g - 1) * 256
    inner = local % 256
    slot = (local // 256) * 8 + ((inner // 32) % 2) * 4 + inner // 64
    place = jnp.where(mask_a[...] == 1, slot * 32 + inner % 32, -1)
    lane24 = grid_index((24, 128), 1)
    for pair in range(16):
        rows = []
        for n in (2 * pair, 2 * pair + 1):
            wide = jnp.broadcast_to(place[:, n : n + 1], (24, 128)) - lane24
            rows.append(jnp.concatenate([flag(wide == 128 * k) for k in range(6)], axis=1))
        pick_a[48 * pair : 48 * pair + 48, :] = jnp.concatenate(rows, axis=0).astype(BF)

    def received(ref, sem):
        pltpu.make_async_copy(ref, ref, sem).wait()

    received(parent_window.at[pl.ds(0, 7)], b_recv.at[0])
    loads[3].wait()
    lifted = []
    for c in range(4):
        one = parent_window[8 + 2 * c].astype(F32)
        two = parent_window[9 + 2 * c].astype(F32)
        children = jnp.concatenate([one[0:8], one[8:16], two[0:8], two[8:16]], axis=1).astype(BF)
        lifted.append(nt(children, v_tc[64 * c : 64 * c + 64, :]))
    grand_window[g] = jnp.concatenate(
        [jnp.concatenate(lifted[0:2], axis=1), jnp.concatenate(lifted[2:4], axis=1)], axis=0
    ).astype(BF)

    def grand_copy(d):
        block = grand_window.at[g]
        return pltpu.make_async_remote_copy(
            src_ref=block,
            dst_ref=block,
            send_sem=c_send.at[0],
            recv_sem=c_recv.at[0],
            device_id={"tel": t, "leaf": lax.rem(g + d, groups)},
            device_id_type=MESH,
        )

    def start_grand(d, carry):
        grand_copy(d).start()
        return carry

    lax.fori_loop(1, groups, start_grand, 0)
    group_parents = parent_window.at[pl.ds(8, 8)]
    sent.append(send(group_parents, parent_window.at[pl.ds(0, 8)], bx_send.at[0], bx_recv.at[0], t, up))
    sent.append(
        send(group_parents, parent_window.at[pl.ds(16, 8)], bx_send.at[1], bx_recv.at[1], t, down)
    )

    for d in range(1, 4):
        source = 8 + core * 4 + lax.rem(y + 4 - d, 4)
        received(leaf_window.at[source], y_recv.at[d - 1])
        spread(source, d)

    choose_b, half_b = [], []
    lane384 = grid_index((8, 384), 1)
    for n in range(4):
        entry = column([lists_b[n : n + 1, :]], 24, 0) - (g - 1) * 32
        valid = column([mask_b[n : n + 1, :]], 24, 0)
        base = jnp.where(valid == 1, (entry // 2) * 8, -1000)
        for i in range(3):
            wide = jnp.broadcast_to(base[8 * i : 8 * i + 8], (8, 384)) - lane384
            choose_b.extend(flag(wide == -r) for r in range(8))
            half_b.append(jnp.broadcast_to(entry[8 * i : 8 * i + 8] % 2, (8, 128)) == lane // 64)
    choose_b = jnp.concatenate(choose_b, axis=0).astype(BF)
    grand_rows = 16 * groups
    entry = column([lists_c[p] for p in range(3)], 16, 4)
    valid = column([mask_c[p] for p in range(3)], 16, 4)
    base = jnp.where(valid == 1, (entry // 2) * 8, -1000)
    wide = jnp.broadcast_to(base, (16, grand_rows)) - grid_index((16, grand_rows), 1)
    choose_c = jnp.concatenate([flag(wide == -r) for r in range(8)], axis=0).astype(BF)
    half_c = jnp.broadcast_to(entry % 2, (16, 128)) == grid_index((16, 128), 1) // 64

    row, col = grid_index((128, 256), 0), grid_index((128, 256), 1)
    same_p = row % 8 == col % 8
    row, col = grid_index((32, 256), 0), grid_index((32, 256), 1)
    fold = flag(
        (row // 16 == col // 128) & (row % 8 == (col // 16) % 8) & ((row // 8) % 2 == (col // 8) % 2)
    ).astype(BF)
    diagonal4 = row // 8 == col // 64
    row, col = grid_index((512, 256), 0), grid_index((512, 256), 1)
    expand = flag(col % 64 == 2 * ((row % 256) // 8) + row // 256).astype(BF)
    row, col = grid_index((32, 128), 0), grid_index((32, 128), 1)
    diagonal2 = (row // 8) % 2 == col // 64
    row, col = grid_index((16, 128), 0), grid_index((16, 128), 1)
    halves = flag(row // 8 == col // 64).astype(BF)

    for d in range(4):
        source = core * 4 + lax.rem(y + 4 - d, 4)
        for side in range(2):
            block = leaf_window.at[source + 16 * side]
            received(block, x_recv.at[4 * side + d])
            k = 4 + 2 * d + side
            sent.append(send(block, block, mate_send.at[k], mate_recv.at[k], mate, g))

    received(grand_window.at[pl.ds(0, groups - 1)], c_recv.at[0])
    loads[4].wait()
    found = nn(choose_c, grand_window[...].reshape(grand_rows, 128))
    lane16 = grid_index((16, 128), 1)
    rows = []
    for r in range(8):
        one = found[16 * r : 16 * r + 16]
        both = jnp.where(half_c, one, pltpu.roll(one, 64, 1))
        rows.append(jnp.where(lane16 < 64, both, 0.0))
        rows.append(jnp.where(lane16 < 64, 0.0, both))
    full = nt(jnp.concatenate(rows, axis=0).astype(BF), v_cc[...])
    row, col = grid_index((256, 512), 0), grid_index((256, 512), 1)
    full = jnp.where(row % 16 == col % 16, full, 0.0).astype(BF)
    row, col = grid_index((64, 256), 0), grid_index((64, 256), 1)
    fold_c = flag(
        (row // 32 == (col // 16) % 2) & ((row // 8) % 4 == col % 4) & (row % 8 == col // 32)
    ).astype(BF)
    folded = nn(fold_c, full).astype(BF)
    row, col = grid_index((512, 128), 0), grid_index((512, 128), 1)
    share = nn(folded[0:32], flag(col % 64 == 2 * (row // 16)).astype(BF)) + nn(
        folded[32:64], flag(col % 64 == 2 * (row // 16) + 1).astype(BF)
    )
    for c in range(4):
        share_out[c] = share[8 * c : 8 * c + 8]
    for d in range(1, 8):
        target = lax.rem(t + d, 8)
        sent.append(
            send(share_out.at[target // 2], share_in.at[d - 1], s_send.at[d - 1], s_recv.at[0], target, g)
        )

    def couple(lhs, coupling):
        wide = jnp.concatenate([coupling[256 * i : 256 * i + 256] for i in range(3)], axis=1)
        return jnp.where(same_p, nt(lhs, wide), 0.0).astype(BF)

    def folded_rows(pair):
        z = nn(fold, jnp.concatenate(pair, axis=0)).astype(F32)
        return [jnp.concatenate([z[16 * j : 16 * j + 8], z[16 * j + 8 : 16 * j + 16]], axis=1) for j in (0, 1)]

    received(parent_window.at[pl.ds(0, 8)], bx_recv.at[0])
    received(parent_window.at[pl.ds(16, 8)], bx_recv.at[1])
    loads[5].wait()
    found = nn(choose_b, parent_window[...].reshape(384, 128))
    rows, pair = [], []
    for n in range(4):
        lanes = []
        for i in range(3):
            pieces = []
            for r in range(8):
                at = 8 * ((n * 3 + i) * 8 + r)
                one = found[at : at + 8]
                both = jnp.where(half_b[n * 3 + i], one, pltpu.roll(one, 64, 1))
                pieces.append(jnp.concatenate([both, both], axis=0).astype(BF) * halves)
            lanes.append(jnp.concatenate(pieces, axis=0))
        pair.append(couple(jnp.concatenate(lanes, axis=1), v_cb[n]))
        if n % 2:
            rows.extend(folded_rows(pair))
            pair = []
    near_b = nn(jnp.concatenate(rows, axis=0).astype(BF), expand[:, 0:128])

    for k in range(4):
        if k == 0:
            block = leaf_window.at[8 + (1 - core) * 4 + y]
        else:
            block = leaf_window.at[8 + (1 - core) * 4 + lax.rem(y + 4 - k, 4)]
        received(block, mate_recv.at[k])
    for d in range(4):
        source = (1 - core) * 4 + lax.rem(y + 4 - d, 4)
        for side in range(2):
            received(leaf_window.at[source + 16 * side], mate_recv.at[4 + 2 * d + side])
    loads[6].wait()
    for half in range(2):
        window = jnp.concatenate(
            [
                leaf_window[:, 32 * k : 32 * k + 32, :].reshape(768, 128)
                for k in (2 * half, 2 * half + 1)
            ],
            axis=1,
        )
        picked[:, 256 * half : 256 * half + 256] = nn(pick_a[...], window)

    def leaf_stack(s, carry):
        rows, pair = [], []
        for j in range(4):
            n = 4 * s + j
            lanes = []
            for i in range(3):
                eight = picked[pl.ds(pl.multiple_of(24 * n + 8 * i, 8), 8), :]
                pieces = []
                for k in range(4):
                    one = eight[:, 128 * k : 128 * k + 128]
                    turned = pltpu.roll(one, 64, 1)
                    pieces.append(jnp.concatenate([one, turned], axis=0).astype(BF) * halves)
                    pieces.append(jnp.concatenate([turned, one], axis=0).astype(BF) * halves)
                lanes.append(jnp.concatenate(pieces, axis=0))
            pair.append(couple(jnp.concatenate(lanes, axis=1), v_ca.at[n]))
            if j % 2:
                rows.extend(folded_rows(pair))
                pair = []
        near[s] = nn(jnp.concatenate(rows, axis=0).astype(BF), expand)
        return carry

    lax.fori_loop(0, 8, leaf_stack, 0)

    received(share_in, s_recv.at[0])
    total = share_out[y]
    for d in range(7):
        total = total + share_in[d]
    y_c = total[:, 0:64].astype(BF)
    spread_c = nn(y_c, v_tc[pl.ds(pl.multiple_of(64 * y, 64), 64), :])
    own_down = jnp.where(core == 0, spread_c[:, 0:256], spread_c[:, 256:512])
    for h in range(2):
        part = own_down[:, 128 * h : 128 * h + 128]
        part = near_b[16 * h : 16 * h + 16] + jnp.concatenate([part, part], axis=0)
        y_b = jnp.where(diagonal2[0:16], part, 0.0).astype(BF)
        spread_b = nn(y_b, v_tb[128 * h : 128 * h + 128, :])
        for j in range(2):
            for k in range(2):
                s = 4 * h + 2 * j + k
                part = spread_b[8 * j : 8 * j + 8, 256 * k : 256 * k + 256]
                part = near[s] + jnp.concatenate([part] * 4, axis=0)
                y_a = jnp.where(diagonal4, part, 0.0).astype(BF)
                field[32 * s : 32 * s + 32, :] = nn(y_a, v_basis[256 * s : 256 * s + 256, :]).astype(BF)

    for copy in sent:
        copy.wait_send()
    pltpu.make_async_copy(
        grand_window.at[pl.ds(0, groups - 1)], grand_window.at[pl.ds(0, groups - 1)], c_send.at[0]
    ).wait()


def tiles(coupling):
    boxes = coupling.shape[0]
    split = coupling.reshape(boxes, 3, 8, 32, 128)
    return split.transpose(0, 1, 3, 2, 4).reshape(boxes, 768, 128)


def on_device(
    values,
    basis,
    transfer_b,
    transfer_c,
    coupling_a,
    lists_a,
    mask_a,
    coupling_b,
    lists_b,
    mask_b,
    coupling_c,
    lists_c,
    mask_c,
):
    groups = lax.axis_size("leaf")
    grand = coupling_c[0].transpose(1, 0, 2).reshape(12, 32, 128)
    grand = jnp.pad(grand, ((0, 4), (0, 0), (0, 0))).transpose(1, 0, 2).reshape(512, 128)
    operands = (
        values.reshape(256, 256),
        basis.reshape(2048, 256),
        transfer_b.reshape(256, 512),
        transfer_c.reshape(256, 512),
        tiles(coupling_a[0]),
        tiles(coupling_b[0]),
        grand,
        lists_a[0].T,
        mask_a[0].T,
        lists_b[0],
        mask_b[0],
        lists_c.transpose(2, 0, 1),
        mask_c.transpose(2, 0, 1),
    )
    anywhere = pl.BlockSpec(memory_space=pl.ANY)
    local = pl.BlockSpec(memory_space=pltpu.VMEM)
    dma = pltpu.SemaphoreType.DMA
    field = pl.pallas_call(
        functools.partial(kernel, groups),
        out_shape=jax.ShapeDtypeStruct((256, 256), BF),
        in_specs=[anywhere] * 7 + [local] * 6,
        out_specs=local,
        scratch_shapes=[pltpu.VMEM(x.shape, x.dtype) for x in operands[:7]]
        + [
            pltpu.VMEM((24, 128, 128), BF),
            pltpu.VMEM((24, 16, 128), BF),
            pltpu.VMEM((groups, 16, 128), BF),
            pltpu.VMEM((4, 8, 128), F32),
            pltpu.VMEM((7, 8, 128), F32),
            pltpu.VMEM((768, 768), BF),
            pltpu.VMEM((768, 512), F32),
            pltpu.VMEM((8, 32, 256), F32),
        ]
        + [dma((k,)) for k in (7, 3, 3, 8, 8, 12, 12, 7, 1, 2, 2, 1, 1, 7, 1)],
        compiler_params=pltpu.CompilerParams(
            collective_id=0, has_side_effects=True, vmem_limit_bytes=40 * 1024 * 1024
        ),
        cost_estimate=pl.CostEstimate(flops=5_000_000_000, bytes_accessed=10_000_000, transcendentals=0),
        name="far_field",
    )(*operands)
    return field.reshape(1, 32, 8, 256)


def solution(mesh):
    in_specs = (
        P("leaf", "tel", None, None),
        P("leaf", "tel", None, None),
        P("leaf", "tel", None, None),
        P("leaf", None, None, None),
        P("leaf", "tel", None, None),
        P("leaf", "tel", None),
        P("leaf", "tel", None),
        P("leaf", "tel", None, None),
        P("leaf", "tel", None),
        P("leaf", "tel", None),
        P("leaf", None, "tel", None),
        P("leaf", None, "tel"),
        P("leaf", None, "tel"),
    )
    out_specs = P("leaf", "tel", None, None)
    return jax.shard_map(
        on_device, mesh=mesh, in_specs=in_specs, out_specs=out_specs, check_vma=False
    )
```

time: 169 us -> 49.6 us (0.29)
  the two profiles are of different devices: /device:TPU:102 before, /device:TPU:1 now
where the time goes in v1:
time: 49.6 us; the launch traced here: 49.1 us
  Pallas kernels  35.2 us (71%)
  local copies, waits for them, and re-layouts  13.8 us (28%)
    pallas_call x1, Pallas kernels, on_device(): pl.pallas_call(functools.partial(kernel, groups), out_shape=jax.ShapeDtyp...  35.2 us
    unnamed x25, local copies, waits for them, and re-layouts  12.7 us
    reshape x2, local copies, waits for them, and re-layouts, on_device(): grand = coupling_c[0].transpose(1, 0, 2).reshape(12, 32, 128)  1.05 us

profile of v1, /device:TPU:1, one launch (start us, length us, event | category | flops | bytes accessed | tf_op | source)
XLA Modules:
  0.0 49.1 jit_solution(2309144538712035078)
XLA Ops:
  0.0 1.0 %reshape.33 = bf16[12,32,128]{2,1,0:T(8,128)(2,1)S(1)} reshape(bf16[3,4,4096]{2,1,0:T(4,128)(2,1)} %bitcast.45) | data formatting | bytes 196608 | tf_op jit(solution)/shard_map/reshape | solution.py:448
  1.1 0.0 copy-start
  1.1 2.8 %copy-done = bf16[1,32,24,4096]{3,2,1,0:T(8,128)(2,1)S(1)} copy-done((bf16[1,32,24,4096]{3,2,1,0:T(8,128)(2,1)S(1)}, bf16[1,32,24,4096]{3,2,1,0:T(8,128)(2,1)}, u32[]{:S(2)}) %copy-start) | copy-done | bytes 6291480
  3.9 0.0 copy-start.1
  3.9 1.2 %copy-done.1 = bf16[1,32,64,256]{3,2,1,0:T(8,128)(2,1)S(1)} copy-done((bf16[1,32,64,256]{3,2,1,0:T(8,128)(2,1)S(1)}, bf16[1,32,64,256]{3,2,1,0:T(8,128)(2,1)}, u32[]{:S(2)}) %copy-start.1) | copy-done | bytes 1048600
  5.1 0.0 copy-start.2
  5.1 1.1 %copy-done.2 = bf16[1,4,24,4096]{3,2,1,0:T(8,128)(2,1)S(1)} copy-done((bf16[1,4,24,4096]{3,2,1,0:T(8,128)(2,1)S(1)}, bf16[1,4,24,4096]{3,2,1,0:T(8,128)(2,1)}, u32[]{:S(2)}) %copy-start.2) | copy-done | bytes 786456
  6.2 0.0 copy-start.3
  6.2 0.9 %copy-done.3 = bf16[1,4,64,512]{3,2,1,0:T(8,128)(2,1)S(1)} copy-done((bf16[1,4,64,512]{3,2,1,0:T(8,128)(2,1)S(1)}, bf16[1,4,64,512]{3,2,1,0:T(8,128)(2,1)}, u32[]{:S(2)}) %copy-start.3) | copy-done | bytes 262168
  7.2 0.9 %copy-done.4 = bf16[1,4,64,512]{3,2,1,0:T(8,128)(2,1)S(1)} copy-done((bf16[1,4,64,512]{3,2,1,0:T(8,128)(2,1)S(1)}, bf16[1,4,64,512]{3,2,1,0:T(8,128)(2,1)}, u32[]{:S(2)}) %copy-start.4) | copy-done | bytes 262168
  8.1 0.0 copy-start.5
  8.1 0.9 %copy-done.5 = bf16[1,32,8,256]{3,2,1,0:T(8,128)(2,1)S(1)} copy-done((bf16[1,32,8,256]{3,2,1,0:T(8,128)(2,1)S(1)}, bf16[1,32,8,256]{3,2,1,0:T(8,128)(2,1)}, u32[]{:S(2)}) %copy-start.5) | copy-done | bytes 131096
  9.1 0.0 copy-start.6
  9.1 0.7 %copy-done.6 = s32[1,32,24]{1,2,0:T(8,128)S(1)} copy-done((s32[1,32,24]{1,2,0:T(8,128)S(1)}, s32[1,32,24]{1,2,0:T(8,128)}, u32[]{:S(2)}) %copy-start.6) | copy-done | bytes 3096
  9.8 0.0 copy-start.7
  9.8 0.7 %copy-done.7 = s32[1,32,24]{1,2,0:T(8,128)S(1)} copy-done((s32[1,32,24]{1,2,0:T(8,128)S(1)}, s32[1,32,24]{1,2,0:T(8,128)}, u32[]{:S(2)}) %copy-start.7) | copy-done | bytes 3096
  10.5 0.7 %copy-done.8 = s32[1,4,24]{2,1,0:T(4,128)S(1)} copy-done((s32[1,4,24]{2,1,0:T(4,128)S(1)}, s32[1,4,24]{2,1,0:T(4,128)}, u32[]{:S(2)}) %copy-start.8) | copy-done | bytes 408
  11.1 0.0 copy-start.9
  11.1 0.7 %copy-done.9 = s32[1,4,24]{2,1,0:T(4,128)S(1)} copy-done((s32[1,4,24]{2,1,0:T(4,128)S(1)}, s32[1,4,24]{2,1,0:T(4,128)}, u32[]{:S(2)}) %copy-start.9) | copy-done | bytes 408
  11.8 0.0 copy-start.10
  11.8 0.7 %copy-done.10 = s32[1,4,3]{1,0,2:T(1,128)S(1)} copy-done((s32[1,4,3]{1,0,2:T(1,128)S(1)}, s32[1,4,3]{1,0,2:T(1,128)}, u32[]{:S(2)}) %copy-start.10) | copy-done | bytes 72
  12.5 0.7 %copy-done.11 = s32[1,4,3]{1,0,2:T(1,128)S(1)} copy-done((s32[1,4,3]{1,0,2:T(1,128)S(1)}, s32[1,4,3]{1,0,2:T(1,128)}, u32[]{:S(2)}) %copy-start.11) | copy-done | bytes 72
  13.2 35.2 %far_field.1 = bf16[256,256]{1,0:T(8,128)(2,1)S(1)} custom-call(bf16[256,256]{1,0:T(8,128)(2,1)S(1)} %bitcast.38, bf16[2048,256]{1,0:T(8,128)(2,1)S(1)} %bitcast.34, bf16[256,512]{1,0:T(8,128)(2,1)S(1)} %bitcast.36, bf16[256,512]{1,0:T(8,128)(2,1)S(1)} %bitcast.37, bf16[32,768,128]{2,1,0:T(8,128)(2,1)S(1)} %bitcast.33, bf16[4,768,128]{2,1,0:T(8,128)(2,1)S(1)} %bitcast.35, ...), custom_call_target="tpu_custom_call" | custom-call | flops 5000000000 | bytes 10000000 | tf_op jit(solution)/shard_map/far_field/pallas_call | solution.py:468
  48.4 0.7 %copy.16 = bf16[1,32,8,256]{3,2,1,0:T(8,128)(2,1)} copy(bf16[1,32,8,256]{3,2,1,0:T(8,128)(2,1)S(1)} %bitcast.32) | data formatting | bytes 262144
  (5 shorter events, 0.1 us)
Async XLA Ops:
  1.1 2.8 %copy-start = (bf16[1,32,24,4096]{3,2,1,0:T(8,128)(2,1)S(1)}, bf16[1,32,24,4096]{3,2,1,0:T(8,128)(2,1)}, u32[]{:S(2)}) copy-start(bf16[1,32,24,4096]{3,2,1,0:T(8,128)(2,1)} %param.17) | copy-start | bytes 18874372
  3.9 1.2 %copy-start.1 = (bf16[1,32,64,256]{3,2,1,0:T(8,128)(2,1)S(1)}, bf16[1,32,64,256]{3,2,1,0:T(8,128)(2,1)}, u32[]{:S(2)}) copy-start(bf16[1,32,64,256]{3,2,1,0:T(8,128)(2,1)} %param.14) | copy-start | bytes 3145732
  5.1 1.1 %copy-start.2 = (bf16[1,4,24,4096]{3,2,1,0:T(8,128)(2,1)S(1)}, bf16[1,4,24,4096]{3,2,1,0:T(8,128)(2,1)}, u32[]{:S(2)}) copy-start(bf16[1,4,24,4096]{3,2,1,0:T(8,128)(2,1)} %param.20) | copy-start | bytes 2359300
  6.2 0.9 %copy-start.3 = (bf16[1,4,64,512]{3,2,1,0:T(8,128)(2,1)S(1)}, bf16[1,4,64,512]{3,2,1,0:T(8,128)(2,1)}, u32[]{:S(2)}) copy-start(bf16[1,4,64,512]{3,2,1,0:T(8,128)(2,1)} %param.15) | copy-start | bytes 786436
  7.2 0.9 %copy-start.4 = (bf16[1,4,64,512]{3,2,1,0:T(8,128)(2,1)S(1)}, bf16[1,4,64,512]{3,2,1,0:T(8,128)(2,1)}, u32[]{:S(2)}) copy-start(bf16[1,4,64,512]{3,2,1,0:T(8,128)(2,1)} %param.16) | copy-start | bytes 786436
  8.1 0.9 %copy-start.5 = (bf16[1,32,8,256]{3,2,1,0:T(8,128)(2,1)S(1)}, bf16[1,32,8,256]{3,2,1,0:T(8,128)(2,1)}, u32[]{:S(2)}) copy-start(bf16[1,32,8,256]{3,2,1,0:T(8,128)(2,1)} %param.13) | copy-start | bytes 393220
  9.1 0.7 %copy-start.6 = (s32[1,32,24]{1,2,0:T(8,128)S(1)}, s32[1,32,24]{1,2,0:T(8,128)}, u32[]{:S(2)}) copy-start(s32[1,32,24]{1,2,0:T(8,128)} %param.18) | copy-start | bytes 9220
  9.8 0.7 %copy-start.7 = (s32[1,32,24]{1,2,0:T(8,128)S(1)}, s32[1,32,24]{1,2,0:T(8,128)}, u32[]{:S(2)}) copy-start(s32[1,32,24]{1,2,0:T(8,128)} %param.19) | copy-start | bytes 9220
  10.5 0.7 %copy-start.8 = (s32[1,4,24]{2,1,0:T(4,128)S(1)}, s32[1,4,24]{2,1,0:T(4,128)}, u32[]{:S(2)}) copy-start(s32[1,4,24]{2,1,0:T(4,128)} %param.21) | copy-start | bytes 1156
  11.1 0.7 %copy-start.9 = (s32[1,4,24]{2,1,0:T(4,128)S(1)}, s32[1,4,24]{2,1,0:T(4,128)}, u32[]{:S(2)}) copy-start(s32[1,4,24]{2,1,0:T(4,128)} %param.22) | copy-start | bytes 1156
  11.8 0.7 %copy-start.10 = (s32[1,4,3]{1,0,2:T(1,128)S(1)}, s32[1,4,3]{1,0,2:T(1,128)}, u32[]{:S(2)}) copy-start(s32[1,4,3]{1,0,2:T(1,128)} %param.24) | copy-start | bytes 148
  12.5 0.7 %copy-start.11 = (s32[1,4,3]{1,0,2:T(1,128)S(1)}, s32[1,4,3]{1,0,2:T(1,128)}, u32[]{:S(2)}) copy-start(s32[1,4,3]{1,0,2:T(1,128)} %param.25) | copy-start | bytes 148

commit v2 on v1

v2 whole, which is shorter than its diff:
```python
import functools

import jax
import jax.numpy as jnp
from jax import lax
from jax.experimental import pallas as pl
from jax.experimental.pallas import tpu as pltpu
from jax.sharding import PartitionSpec as P

BF = jnp.bfloat16
F32 = jnp.float32
MESH = pl.DeviceIdType.MESH


def nt(a, b):
    return lax.dot_general(a, b, (((1,), (1,)), ((), ())), preferred_element_type=F32)


def nn(a, b):
    return jnp.dot(a, b, preferred_element_type=F32)


def grid_index(shape, dim):
    return lax.broadcasted_iota(jnp.int32, shape, dim)


def flag(condition):
    return jnp.where(condition, 1.0, 0.0)


def far_first(depth):
    offsets = [(dz, dx) for dz in range(depth) for dx in range(4) if dz or dx]
    return sorted(offsets, key=lambda o: -(min(o[0], depth - o[0]) + min(o[1], 4 - o[1])))


def column(rows, height, stride):
    sub, lane = grid_index((height, 128), 0), grid_index((height, 128), 1)
    total = jnp.zeros((height, 128), F32)
    for place, row in enumerate(rows):
        width = row.shape[1]
        wide = jnp.concatenate([row.astype(F32), jnp.zeros((1, 128 - width), F32)], axis=1)
        hit = (lane == sub - place * stride) & (lane < width)
        total = total + jnp.where(hit, jnp.broadcast_to(wide, (height, 128)), 0.0)
    return jnp.sum(total, axis=1, keepdims=True).astype(jnp.int32)


def kernel(
    groups,
    values,
    basis,
    transfer_b,
    transfer_c,
    coupling_a,
    coupling_b,
    coupling_c,
    lists_a,
    mask_a,
    lists_b,
    mask_b,
    lists_c,
    mask_c,
    field,
    v_values,
    v_basis,
    v_tb,
    v_tc,
    v_ca,
    v_cb,
    v_cc,
    v_lists_a,
    v_mask_a,
    v_lists_b,
    v_mask_b,
    v_lists_c,
    v_mask_c,
    leaf_window,
    parent_window,
    grand_window,
    share_out,
    share_in,
    pick_a,
    picked,
    left_side,
    products,
    folded,
    near,
    load_sem,
    y_send,
    y_recv,
    x_send,
    x_recv,
    mate_send,
    mate_recv,
    b_send,
    b_recv,
    bx_send,
    bx_recv,
    c_send,
    c_recv,
    here,
    s_send,
    s_recv,
):
    g = lax.axis_index("leaf")
    t = lax.axis_index("tel")
    y, core = t // 2, t % 2
    depth = groups // 4

    def group_at(dz, dx):
        return lax.rem(g // 4 + dz, depth) * 4 + lax.rem(g + dx, 4)

    up, down = lax.rem(g + 1, groups), lax.rem(g + groups - 1, groups)

    loads = [
        pltpu.make_async_copy(source, target, load_sem.at[place])
        for place, (source, target) in enumerate(
            (
                (values, v_values),
                (basis, v_basis),
                (transfer_b, v_tb),
                (transfer_c, v_tc),
                (coupling_c, v_cc),
                (coupling_b, v_cb),
                (coupling_a, v_ca),
                (lists_a, v_lists_a),
                (mask_a, v_mask_a),
                (lists_b, v_lists_b),
                (mask_b, v_mask_b),
                (lists_c, v_lists_c),
                (mask_c, v_mask_c),
            )
        )
    ]
    for load in loads[0:3]:
        load.start()

    barrier = pltpu.get_barrier_semaphore()

    def greet_group(d, carry):
        pl.semaphore_signal(
            barrier, inc=1, device_id={"tel": lax.rem(t + d, 8), "leaf": g}, device_id_type=MESH
        )
        return carry

    lax.fori_loop(1, 8, greet_group, 0)
    z = g // 4

    def signal_plane(semaphore, offset, along_x):
        @pl.when((z + offset >= 0) & (z + offset < depth))
        def _():
            for dx in along_x:
                target = (z + offset) * 4 + lax.rem(g + dx, 4)
                pl.semaphore_signal(
                    semaphore, inc=1, device_id={"tel": t, "leaf": target}, device_id_type=MESH
                )

    def planes(*offsets):
        return sum(((z + o >= 0) & (z + o < depth)).astype(jnp.int32) for o in offsets)

    signal_plane(barrier, 0, (1, 2, 3))
    signal_plane(barrier, 1, range(4))
    signal_plane(barrier, -1, range(4))

    sub, lane = grid_index((8, 128), 0), grid_index((8, 128), 1)
    left = lane < 64
    even_left = (sub % 2 == 0) & left
    odd_right = (sub % 2 == 1) & (lane >= 64)

    for end, first in ((0, 0), (groups - 1, 16)):

        @pl.when(g == end)
        def _():
            leaf_window[first : first + 8] = jnp.zeros((8, 128, 128), BF)
            parent_window[first : first + 8] = jnp.zeros((8, 16, 128), BF)

    loads[0].wait()
    loads[1].wait()
    for load in loads[7:13] + loads[3:7]:
        load.start()
    pl.semaphore_wait(barrier, 10 + 4 * planes(-1, 1))
    for offset in (-1, 1):
        signal_plane(here.at[0], offset, (0,))

    placed, stacked = [], []
    for s in range(8):
        product = nt(v_values[32 * s : 32 * s + 32, :], v_basis[256 * s : 256 * s + 256, :])
        for h in range(2):
            first = product[16 * h : 16 * h + 8, 128 * h : 128 * h + 128]
            second = product[16 * h + 8 : 16 * h + 16, 128 * h : 128 * h + 128]
            placed.append(
                jnp.where(even_left, first, jnp.where(odd_right, pltpu.roll(first, 64, 1), 0.0))
            )
            placed.append(
                jnp.where(even_left, pltpu.roll(second, 64, 1), jnp.where(odd_right, second, 0.0))
            )
            stacked.append(jnp.where(left, first, second))
    placed = jnp.concatenate(placed, axis=0).astype(BF)
    row, col = grid_index((128, 256), 0), grid_index((128, 256), 1)
    order = flag((row % 32 == col // 8) & (row // 32 == (col % 8) // 2)).astype(BF)
    own_slot = 8 + core * 4 + y
    leaf_window[own_slot] = nn(order, placed).astype(BF)

    loads[2].wait()
    lifted = []
    for b in range(4):
        children = jnp.concatenate(stacked[4 * b : 4 * b + 4], axis=1).astype(BF)
        lifted.append(nt(children, v_tb[64 * b : 64 * b + 64, :]))
    parent_window[8 + t] = jnp.concatenate(
        [jnp.concatenate(lifted[0:2], axis=1), jnp.concatenate(lifted[2:4], axis=1)], axis=0
    ).astype(BF)

    def send(source, target, send_sem, recv_sem, tel, leaf, when=True):
        copy = pltpu.make_async_remote_copy(
            src_ref=source,
            dst_ref=target,
            send_sem=send_sem,
            recv_sem=recv_sem,
            device_id={"tel": tel, "leaf": leaf},
            device_id_type=MESH,
        )
        pl.when(when)(copy.start)
        return copy, when

    sent = []
    for d in range(1, 8):
        block = parent_window.at[8 + t]
        sent.append(send(block, block, b_send.at[d - 1], b_recv.at[0], lax.rem(t + d, 8), g))

    mate = t + 1 - 2 * core

    has_up, has_down = g < groups - 1, g > 0

    def spread(slot, place):
        block = leaf_window.at[slot]
        sent.append(
            send(block, leaf_window.at[slot - 8], x_send.at[place], x_recv.at[place], t, up, has_up)
        )
        sent.append(
            send(
                block, leaf_window.at[slot + 8], x_send.at[4 + place], x_recv.at[4 + place], t, down, has_down
            )
        )
        sent.append(send(block, block, mate_send.at[place], mate_recv.at[place], mate, g))

    own = leaf_window.at[own_slot]
    for d in range(1, 4):
        sent.append(
            send(own, own, y_send.at[d - 1], y_recv.at[d - 1], lax.rem(y + d, 4) * 2 + core, g)
        )
    spread(own_slot, 0)

    pl.semaphore_wait(here.at[0], planes(-1, 1))
    for offset in (-2, 2):
        signal_plane(here.at[1], offset, (0,))

    loads[7].wait()
    loads[8].wait()
    local = v_lists_a[...] - (g - 1) * 256
    inner = local % 256
    slot = (local // 256) * 8 + ((inner // 32) % 2) * 4 + inner // 64
    place = jnp.where(v_mask_a[...] == 1, slot * 32 + inner % 32, -1)
    lane24 = grid_index((24, 128), 1)
    for pair in range(16):
        rows = []
        for n in (2 * pair, 2 * pair + 1):
            wide = jnp.broadcast_to(place[:, n : n + 1], (24, 128)) - lane24
            rows.append(jnp.concatenate([flag(wide == 128 * k) for k in range(6)], axis=1))
        pick_a[48 * pair : 48 * pair + 48, :] = jnp.concatenate(rows, axis=0).astype(BF)

    def received(ref, sem, when=True):
        pl.when(when)(pltpu.make_async_copy(ref, ref, sem).wait)

    received(parent_window.at[pl.ds(0, 7)], b_recv.at[0])
    loads[3].wait()
    lifted = []
    for c in range(4):
        one = parent_window[8 + 2 * c].astype(F32)
        two = parent_window[9 + 2 * c].astype(F32)
        children = jnp.concatenate([one[0:8], one[8:16], two[0:8], two[8:16]], axis=1).astype(BF)
        lifted.append(nt(children, v_tc[64 * c : 64 * c + 64, :]))
    grand_window[g] = jnp.concatenate(
        [jnp.concatenate(lifted[0:2], axis=1), jnp.concatenate(lifted[2:4], axis=1)], axis=0
    ).astype(BF)

    block = grand_window.at[g]
    grand_copies = [
        pltpu.make_async_remote_copy(
            src_ref=block,
            dst_ref=block,
            send_sem=c_send.at[k],
            recv_sem=c_recv.at[0],
            device_id={"tel": t, "leaf": group_at(dz, dx)},
            device_id_type=MESH,
        )
        for k, (dz, dx) in enumerate(far_first(depth))
    ]
    sent.extend((copy, True) for copy in grand_copies)

    def send_grand():
        pl.semaphore_wait(here.at[2], planes(-4, 4))
        for copy in grand_copies:
            copy.start()

    group_parents = parent_window.at[pl.ds(8, 8)]
    sent.append(
        send(group_parents, parent_window.at[pl.ds(0, 8)], bx_send.at[0], bx_recv.at[0], t, up, has_up)
    )
    sent.append(
        send(group_parents, parent_window.at[pl.ds(16, 8)], bx_send.at[1], bx_recv.at[1], t, down, has_down)
    )

    for d in range(1, 4):
        source = 8 + core * 4 + lax.rem(y + 4 - d, 4)
        received(leaf_window.at[source], y_recv.at[d - 1])
        spread(source, d)

    pl.semaphore_wait(here.at[1], planes(-2, 2))
    for offset in (-4, 4):
        signal_plane(here.at[2], offset, (0,))
    pl.when(z >= depth // 2)(send_grand)

    for load in loads[9:13]:
        load.wait()
    choose_b, half_b = [], []
    lane384 = grid_index((8, 384), 1)
    for n in range(4):
        entry = column([v_lists_b[n : n + 1, :]], 24, 0) - (g - 1) * 32
        valid = column([v_mask_b[n : n + 1, :]], 24, 0)
        base = jnp.where(valid == 1, (entry // 2) * 8, -1000)
        for i in range(3):
            wide = jnp.broadcast_to(base[8 * i : 8 * i + 8], (8, 384)) - lane384
            choose_b.extend(flag(wide == -r) for r in range(8))
            half_b.append(jnp.broadcast_to(entry[8 * i : 8 * i + 8] % 2, (8, 128)) == lane // 64)
    choose_b = jnp.concatenate(choose_b, axis=0).astype(BF)

    for d in range(4):
        source = core * 4 + lax.rem(y + 4 - d, 4)
        for side in range(2):
            block = leaf_window.at[source + 16 * side]
            there = (has_down, has_up)[side]
            received(block, x_recv.at[4 * side + d], there)
            k = 4 + 2 * d + side
            sent.append(send(block, block, mate_send.at[k], mate_recv.at[k], mate, g, there))

    pl.when(z < depth // 2)(send_grand)

    loads[4].wait()
    codes = jnp.zeros((4, 128), F32)
    lane4 = grid_index((4, 128), 1)
    for p in range(3):
        entry = column([v_lists_c[p]], 4, 0)
        valid = column([v_mask_c[p]], 4, 0)
        code = jnp.where(valid == 1, entry, -1).astype(F32)
        codes = jnp.where(lane4 == p, jnp.broadcast_to(code, (4, 128)), codes)
    codes = jnp.concatenate([codes, jnp.zeros((4, 4096 - 128), F32)], axis=1)
    upper = jnp.concatenate([v_cc[0].astype(F32), v_cc[1].astype(F32)], axis=0)
    lower = jnp.concatenate([v_cc[2].astype(F32), codes], axis=0)
    blocks_c = []
    for k in range(32):
        blocks_c.append(upper[:, 128 * k : 128 * k + 128])
        blocks_c.append(lower[:, 128 * k : 128 * k + 128])
    blocks_c = jnp.concatenate(blocks_c, axis=0).astype(BF)
    row, col = grid_index((512, 512), 0), grid_index((512, 512), 1)
    regroup = flag((row // 128 == col % 4) & (row % 4 == (col % 16) // 4) & ((row % 128) // 4 == col // 16))
    blocks_c = nn(regroup.astype(BF), blocks_c).astype(BF)
    for c in range(4):
        share_out[c] = blocks_c[128 * c : 128 * c + 128]
    share_in[t] = share_out[y]
    for d in range(1, 8):
        target = lax.rem(t + d, 8)
        sent.append(
            send(share_out.at[target // 2], share_in.at[t], s_send.at[d - 1], s_recv.at[0], target, g)
        )

    row, col = grid_index((128, 256), 0), grid_index((128, 256), 1)
    same_p = row % 8 == col % 8
    row, col = grid_index((32, 256), 0), grid_index((32, 256), 1)
    fold = flag(
        ((row // 8) % 2 == col // 128) & (row % 8 == (col // 16) % 8) & (row // 16 == (col // 8) % 2)
    ).astype(BF)
    diagonal4 = row // 8 == col // 64
    row, col = grid_index((512, 256), 0), grid_index((512, 256), 1)
    expand = flag(col % 64 == 2 * ((row % 256) // 8) + row // 256).astype(BF)
    row, col = grid_index((32, 128), 0), grid_index((32, 128), 1)
    diagonal2 = (row // 8) % 2 == col // 64
    row, col = grid_index((16, 128), 0), grid_index((16, 128), 1)
    halves = flag(row // 8 == col // 64).astype(BF)

    def couple(lhs, coupling):
        wide = jnp.concatenate([coupling[256 * i : 256 * i + 256] for i in range(3)], axis=1)
        return jnp.where(same_p, nt(lhs, wide), 0.0).astype(BF)

    def fold_pair(pair):
        both = nn(fold, pair)
        return jnp.concatenate([both[0:16], both[16:32]], axis=1).astype(BF)

    received(parent_window.at[pl.ds(0, 8)], bx_recv.at[0], has_down)
    received(parent_window.at[pl.ds(16, 8)], bx_recv.at[1], has_up)
    loads[5].wait()
    found = nn(choose_b, parent_window[...].reshape(384, 128))
    rows, pair = [], []
    for n in range(4):
        lanes = []
        for i in range(3):
            pieces = []
            for r in range(8):
                at = 8 * ((n * 3 + i) * 8 + r)
                one = found[at : at + 8]
                both = jnp.where(half_b[n * 3 + i], one, pltpu.roll(one, 64, 1))
                pieces.append(jnp.concatenate([both, both], axis=0).astype(BF) * halves)
            lanes.append(jnp.concatenate(pieces, axis=0))
        pair.append(couple(jnp.concatenate(lanes, axis=1), v_cb[n]))
        if n % 2:
            rows.append(fold_pair(jnp.concatenate(pair, axis=0)))
            pair = []
    near_b = nn(jnp.concatenate(rows, axis=0), expand[:, 0:128])

    for k in range(4):
        if k == 0:
            block = leaf_window.at[8 + (1 - core) * 4 + y]
        else:
            block = leaf_window.at[8 + (1 - core) * 4 + lax.rem(y + 4 - k, 4)]
        received(block, mate_recv.at[k])
    for d in range(4):
        source = (1 - core) * 4 + lax.rem(y + 4 - d, 4)
        for side in range(2):
            received(
                leaf_window.at[source + 16 * side], mate_recv.at[4 + 2 * d + side], (has_down, has_up)[side]
            )
    loads[6].wait()
    for half in range(2):
        window = jnp.concatenate(
            [
                leaf_window[:, 32 * k : 32 * k + 32, :].reshape(768, 128)
                for k in (2 * half, 2 * half + 1)
            ],
            axis=1,
        )
        picked[:, 256 * half : 256 * half + 256] = nn(pick_a[...], window)

    def build(n, carry):
        lanes = []
        for i in range(3):
            eight = picked[pl.ds(pl.multiple_of(24 * n + 8 * i, 8), 8), :]
            pieces = []
            for k in range(4):
                one = eight[:, 128 * k : 128 * k + 128]
                turned = pltpu.roll(one, 64, 1)
                pieces.append(jnp.concatenate([one, turned], axis=0).astype(BF) * halves)
                pieces.append(jnp.concatenate([turned, one], axis=0).astype(BF) * halves)
            lanes.append(jnp.concatenate(pieces, axis=0))
        left_side[n] = jnp.concatenate(lanes, axis=1)
        return carry

    def multiply(n, carry):
        products[n] = couple(left_side[n], v_ca.at[n])
        return carry

    def fold_products(pair, carry):
        rows = products[pl.ds(2 * pair, 2)].reshape(256, 256)
        folded[pl.ds(pl.multiple_of(16 * pair, 16), 16), :] = fold_pair(rows)
        return carry

    lax.fori_loop(0, 32, build, 0, unroll=4)
    lax.fori_loop(0, 32, multiply, 0, unroll=4)
    lax.fori_loop(0, 16, fold_products, 0, unroll=4)
    near[...] = nn(folded[...], expand)

    received(share_in.at[pl.ds(0, 7)], s_recv.at[0])
    grand_rows = 16 * groups
    row, lane32 = grid_index((32, 128), 0), grid_index((32, 128), 1)
    choose_c, half_c = [], []
    for source in range(8):
        code = jnp.broadcast_to(share_in[source, 0:16, :].astype(F32)[3:4], (32, 128))
        code = jnp.sum(jnp.where(lane32 == row // 8, code, 0.0), axis=1, keepdims=True).astype(jnp.int32)
        row1 = grid_index((32, 1), 0)
        base = jnp.where((code >= 0) & (row1 < 24), (code // 2) * 8 + row1 % 8, -1000)
        hit = jnp.broadcast_to(base, (32, grand_rows)) == grid_index((32, grand_rows), 1)
        choose_c.append(flag(hit))
        half_c.append(jnp.broadcast_to(code % 2, (32, 128)) == lane32 // 64)
    choose_c = jnp.concatenate(choose_c, axis=0).astype(BF)
    half_c = jnp.concatenate(half_c, axis=0)
    blocks_c = jnp.concatenate([share_in[source] for source in range(8)], axis=1)
    row, col = grid_index((64, 128), 0), grid_index((64, 128), 1)
    same_c = row // 16 == col % 4
    row, col = grid_index((256, 64), 0), grid_index((256, 64), 1)
    expand_c = flag(col == 2 * ((row % 128) // 4) + row // 128).astype(BF)

    received(grand_window.at[pl.ds(0, groups - 1)], c_recv.at[0])
    found = nn(choose_c, grand_window[...].reshape(grand_rows, 128))
    found = jnp.where(half_c, found, pltpu.roll(found, 64, 1))
    lanes = []
    for source in range(8):
        pieces = []
        for e in range(4):
            one = found[32 * source + 8 * e : 32 * source + 8 * e + 8]
            pieces.append(jnp.concatenate([one, one], axis=0).astype(BF) * halves)
        lanes.append(jnp.concatenate(pieces, axis=0))
    full = jnp.where(same_c, nt(jnp.concatenate(lanes, axis=1), blocks_c), 0.0)
    full = full[0:16] + full[16:32] + full[32:48] + full[48:64]
    y_c = nn(jnp.concatenate([full[0:8], full[8:16]], axis=1).astype(BF), expand_c).astype(BF)

    spread_c = nn(y_c, v_tc[pl.ds(pl.multiple_of(64 * y, 64), 64), :])
    own_down = jnp.where(core == 0, spread_c[:, 0:256], spread_c[:, 256:512])
    for h in range(2):
        part = own_down[:, 128 * h : 128 * h + 128]
        part = near_b[16 * h : 16 * h + 16] + jnp.concatenate([part, part], axis=0)
        y_b = jnp.where(diagonal2[0:16], part, 0.0).astype(BF)
        spread_b = nn(y_b, v_tb[128 * h : 128 * h + 128, :])
        for j in range(2):
            for k in range(2):
                s = 4 * h + 2 * j + k
                part = spread_b[8 * j : 8 * j + 8, 256 * k : 256 * k + 256]
                part = near[32 * s : 32 * s + 32, :] + jnp.concatenate([part] * 4, axis=0)
                y_a = jnp.where(diagonal4, part, 0.0).astype(BF)
                field[32 * s : 32 * s + 32, :] = nn(y_a, v_basis[256 * s : 256 * s + 256, :]).astype(BF)

    for copy, when in sent:
        pl.when(when)(copy.wait_send)


def tiles(coupling):
    boxes = coupling.shape[0]
    split = coupling.reshape(boxes, 3, 8, 32, 128)
    return split.transpose(0, 1, 3, 2, 4).reshape(boxes, 768, 128)


def on_device(
    values,
    basis,
    transfer_b,
    transfer_c,
    coupling_a,
    lists_a,
    mask_a,
    coupling_b,
    lists_b,
    mask_b,
    coupling_c,
    lists_c,
    mask_c,
):
    groups = lax.axis_size("leaf")
    operands = (
        values.reshape(256, 256),
        basis.reshape(2048, 256),
        transfer_b.reshape(256, 512),
        transfer_c.reshape(256, 512),
        tiles(coupling_a[0]),
        tiles(coupling_b[0]),
        coupling_c[0].transpose(1, 0, 2),
        lists_a[0].T,
        mask_a[0].T,
        lists_b[0],
        mask_b[0],
        lists_c.transpose(2, 0, 1),
        mask_c.transpose(2, 0, 1),
    )
    far = pl.BlockSpec(memory_space=pltpu.HBM)
    local = pl.BlockSpec(memory_space=pltpu.VMEM)
    dma = pltpu.SemaphoreType.DMA
    field = pl.pallas_call(
        functools.partial(kernel, groups),
        out_shape=jax.ShapeDtypeStruct((256, 256), BF),
        in_specs=[far] * 13,
        out_specs=local,
        scratch_shapes=[pltpu.VMEM(x.shape, x.dtype) for x in operands]
        + [
            pltpu.VMEM((24, 128, 128), BF),
            pltpu.VMEM((24, 16, 128), BF),
            pltpu.VMEM((groups, 16, 128), BF),
            pltpu.VMEM((4, 128, 128), BF),
            pltpu.VMEM((8, 128, 128), BF),
            pltpu.VMEM((768, 768), BF),
            pltpu.VMEM((768, 512), F32),
            pltpu.VMEM((32, 128, 384), BF),
            pltpu.VMEM((32, 128, 256), BF),
            pltpu.VMEM((256, 512), BF),
            pltpu.VMEM((256, 256), F32),
        ]
        + [dma((k,)) for k in (13, 3, 3, 8, 8, 12, 12, 7, 1, 2, 2, groups - 1, 1)]
        + [pltpu.SemaphoreType.REGULAR((3,)), dma((7,)), dma((1,))],
        compiler_params=pltpu.CompilerParams(
            collective_id=0, has_side_effects=True, vmem_limit_bytes=60 * 1024 * 1024
        ),
        cost_estimate=pl.CostEstimate(flops=5_000_000_000, bytes_accessed=10_000_000, transcendentals=0),
        name="far_field",
    )(*operands)
    return field.reshape(1, 32, 8, 256)


def solution(mesh):
    in_specs = (
        P("leaf", "tel", None, None),
        P("leaf", "tel", None, None),
        P("leaf", "tel", None, None),
        P("leaf", None, None, None),
        P("leaf", "tel", None, None),
        P("leaf", "tel", None),
        P("leaf", "tel", None),
        P("leaf", "tel", None, None),
        P("leaf", "tel", None),
        P("leaf", "tel", None),
        P("leaf", None, "tel", None),
        P("leaf", None, "tel"),
        P("leaf", None, "tel"),
    )
    out_specs = P("leaf", "tel", None, None)
    return jax.shard_map(
        on_device, mesh=mesh, in_specs=in_specs, out_specs=out_specs, check_vma=False
    )
```

time: 49.6 us -> 30.5 us (0.61)
  the two profiles are of different devices: /device:TPU:1 before, /device:TPU:102 now
where the time goes in v2:
time: 30.5 us; the launch traced here: 30.1 us
  Pallas kernels  28.6 us (94%)
  local copies, waits for them, and re-layouts  1.57 us (5%)
    pallas_call x1, Pallas kernels, on_device(): pl.pallas_call(functools.partial(kernel, groups), out_shape=jax.ShapeDtyp...  28.6 us
    unnamed x1, local copies, waits for them, and re-layouts  1.57 us

profile of v2, /device:TPU:102, one launch (start us, length us, event | category | flops | bytes accessed | tf_op | source)
XLA Modules:
  0.0 30.1 jit_solution(9379716436056582504)
XLA Ops:
  0.0 28.6 %far_field.1 = bf16[256,256]{1,0:T(8,128)(2,1)} custom-call(bf16[256,256]{1,0:T(8,128)(2,1)} %bitcast.34, bf16[2048,256]{1,0:T(8,128)(2,1)} %bitcast.30, bf16[256,512]{1,0:T(8,128)(2,1)} %bitcast.32, bf16[256,512]{1,0:T(8,128)(2,1)} %bitcast.33, bf16[32,768,128]{2,1,0:T(8,128)(2,1)} %bitcast.29, bf16[4,768,128]{2,1,0:T(8,128)(2,1)} %bitcast.31, ...), custom_call_target="tpu_custom_call" | custom-call | flops 5000000000 | bytes 10000000 | tf_op jit(solution)/shard_map/far_field/pallas_call | solution.py:562
  28.6 1.6 %copy.15 = bf16[1,32,8,256]{3,2,1,0:T(8,128)(2,1)} copy(bf16[1,32,8,256]{3,2,1,0:T(8,128)(2,1)} %bitcast.28) | data formatting | bytes 262144

commit v3 on v2

--- a/solution.py
+++ b/solution.py
@@ -59,7 +59,7 @@
     mask_b,
     lists_c,
     mask_c,
-    field,
+    out,
     v_values,
     v_basis,
     v_tb,
@@ -84,6 +84,8 @@
     products,
     folded,
     near,
+    field,
+    out_sem,
     load_sem,
     y_send,
     y_recv,
@@ -143,23 +145,34 @@
         return carry
 
     lax.fori_loop(1, 8, greet_group, 0)
-    z = g // 4
-
-    def signal_plane(semaphore, offset, along_x):
-        @pl.when((z + offset >= 0) & (z + offset < depth))
+    half = groups // 2
+    z, upper_half = g // 4, g >= half
+    lower_half = jnp.logical_not(upper_half)
+
+    def signal(semaphore, target):
+        pl.semaphore_signal(
+            semaphore, inc=1, device_id={"tel": t, "leaf": target}, device_id_type=MESH
+        )
+
+    def signal_plane(offset, along_x, when):
+        @pl.when(when)
         def _():
             for dx in along_x:
-                target = (z + offset) * 4 + lax.rem(g + dx, 4)
-                pl.semaphore_signal(
-                    semaphore, inc=1, device_id={"tel": t, "leaf": target}, device_id_type=MESH
-                )
-
-    def planes(*offsets):
-        return sum(((z + o >= 0) & (z + o < depth)).astype(jnp.int32) for o in offsets)
-
-    signal_plane(barrier, 0, (1, 2, 3))
-    signal_plane(barrier, 1, range(4))
-    signal_plane(barrier, -1, range(4))
+                signal(barrier, (z + offset) * 4 + lax.rem(g + dx, 4))
+
+    def signal_half(semaphore, start, when):
+        def one(d, carry):
+            signal(semaphore, start + lax.rem(g + d, half))
+            return carry
+
+        @pl.when(when)
+        def _():
+            lax.fori_loop(0, half, one, 0)
+
+    signal_half(barrier, half, lower_half)
+    signal_plane(0, (1, 2, 3), True)
+    signal_plane(1, range(4), (z < depth - 1) & (z != depth // 2 - 1))
+    signal_plane(-1, range(4), z > 0)
 
     sub, lane = grid_index((8, 128), 0), grid_index((8, 128), 1)
     left = lane < 64
@@ -173,14 +186,16 @@
             leaf_window[first : first + 8] = jnp.zeros((8, 128, 128), BF)
             parent_window[first : first + 8] = jnp.zeros((8, 16, 128), BF)
 
+    beside = (z > 0).astype(jnp.int32) + (z < depth - 1).astype(jnp.int32)
+    beside = beside - (z == depth // 2).astype(jnp.int32)
+    pl.semaphore_wait(barrier, 10 + 4 * beside + half * upper_half.astype(jnp.int32))
+    signal_half(here.at[0], 0, upper_half)
+    pl.when(upper_half & (z < depth - 1))(lambda: signal(here.at[1], g + 4))
+    pl.when(upper_half & (z > depth // 2))(lambda: signal(here.at[1], g - 4))
     loads[0].wait()
     loads[1].wait()
     for load in loads[7:13] + loads[3:7]:
         load.start()
-    pl.semaphore_wait(barrier, 10 + 4 * planes(-1, 1))
-    for offset in (-1, 1):
-        signal_plane(here.at[0], offset, (0,))
-
     placed, stacked = [], []
     for s in range(8):
         product = nt(v_values[32 * s : 32 * s + 32, :], v_basis[256 * s : 256 * s + 256, :])
@@ -195,8 +210,9 @@
             )
             stacked.append(jnp.where(left, first, second))
     placed = jnp.concatenate(placed, axis=0).astype(BF)
-    row, col = grid_index((128, 256), 0), grid_index((128, 256), 1)
-    order = flag((row % 32 == col // 8) & (row // 32 == (col % 8) // 2)).astype(BF)
+    row = grid_index((128, 1), 0)
+    first = (row % 32) * 8 + (row // 32) * 2
+    order = flag(jnp.broadcast_to(first, (128, 256)) == (grid_index((128, 256), 1) & -2)).astype(BF)
     own_slot = 8 + core * 4 + y
     leaf_window[own_slot] = nn(order, placed).astype(BF)
 
@@ -249,9 +265,13 @@
         )
     spread(own_slot, 0)
 
-    pl.semaphore_wait(here.at[0], planes(-1, 1))
-    for offset in (-2, 2):
-        signal_plane(here.at[1], offset, (0,))
+    @pl.when(upper_half)
+    def _():
+        pl.semaphore_wait(here.at[1], 1 + ((z > depth // 2) & (z < depth - 1)).astype(jnp.int32))
+        signal(here.at[2], jnp.where(z < depth // 2 + 2, g + 8, g - 8))
+
+    def received(ref, sem, when=True):
+        pl.when(when)(pltpu.make_async_copy(ref, ref, sem).wait)
 
     loads[7].wait()
     loads[8].wait()
@@ -267,8 +287,10 @@
             rows.append(jnp.concatenate([flag(wide == 128 * k) for k in range(6)], axis=1))
         pick_a[48 * pair : 48 * pair + 48, :] = jnp.concatenate(rows, axis=0).astype(BF)
 
-    def received(ref, sem, when=True):
-        pl.when(when)(pltpu.make_async_copy(ref, ref, sem).wait)
+    for d in range(1, 4):
+        source = 8 + core * 4 + lax.rem(y + 4 - d, 4)
+        received(leaf_window.at[source], y_recv.at[d - 1])
+        spread(source, d)
 
     received(parent_window.at[pl.ds(0, 7)], b_recv.at[0])
     loads[3].wait()
@@ -296,10 +318,12 @@
     ]
     sent.extend((copy, True) for copy in grand_copies)
 
-    def send_grand():
-        pl.semaphore_wait(here.at[2], planes(-4, 4))
+    def send_grand(semaphore, count):
+        pl.semaphore_wait(semaphore, count)
         for copy in grand_copies:
             copy.start()
+
+    pl.when(upper_half)(lambda: send_grand(here.at[2], 1))
 
     group_parents = parent_window.at[pl.ds(8, 8)]
     sent.append(
@@ -309,42 +333,9 @@
         send(group_parents, parent_window.at[pl.ds(16, 8)], bx_send.at[1], bx_recv.at[1], t, down, has_down)
     )
 
-    for d in range(1, 4):
-        source = 8 + core * 4 + lax.rem(y + 4 - d, 4)
-        received(leaf_window.at[source], y_recv.at[d - 1])
-        spread(source, d)
-
-    pl.semaphore_wait(here.at[1], planes(-2, 2))
-    for offset in (-4, 4):
-        signal_plane(here.at[2], offset, (0,))
-    pl.when(z >= depth // 2)(send_grand)
-
+    loads[4].wait()
     for load in loads[9:13]:
         load.wait()
-    choose_b, half_b = [], []
-    lane384 = grid_index((8, 384), 1)
-    for n in range(4):
-        entry = column([v_lists_b[n : n + 1, :]], 24, 0) - (g - 1) * 32
-        valid = column([v_mask_b[n : n + 1, :]], 24, 0)
-        base = jnp.where(valid == 1, (entry // 2) * 8, -1000)
-        for i in range(3):
-            wide = jnp.broadcast_to(base[8 * i : 8 * i + 8], (8, 384)) - lane384
-            choose_b.extend(flag(wide == -r) for r in range(8))
-            half_b.append(jnp.broadcast_to(entry[8 * i : 8 * i + 8] % 2, (8, 128)) == lane // 64)
-    choose_b = jnp.concatenate(choose_b, axis=0).astype(BF)
-
-    for d in range(4):
-        source = core * 4 + lax.rem(y + 4 - d, 4)
-        for side in range(2):
-            block = leaf_window.at[source + 16 * side]
-            there = (has_down, has_up)[side]
-            received(block, x_recv.at[4 * side + d], there)
-            k = 4 + 2 * d + side
-            sent.append(send(block, block, mate_send.at[k], mate_recv.at[k], mate, g, there))
-
-    pl.when(z < depth // 2)(send_grand)
-
-    loads[4].wait()
     codes = jnp.zeros((4, 128), F32)
     lane4 = grid_index((4, 128), 1)
     for p in range(3):
@@ -360,17 +351,52 @@
         blocks_c.append(upper[:, 128 * k : 128 * k + 128])
         blocks_c.append(lower[:, 128 * k : 128 * k + 128])
     blocks_c = jnp.concatenate(blocks_c, axis=0).astype(BF)
-    row, col = grid_index((512, 512), 0), grid_index((512, 512), 1)
-    regroup = flag((row // 128 == col % 4) & (row % 4 == (col % 16) // 4) & ((row % 128) // 4 == col // 16))
+    row = grid_index((512, 1), 0)
+    source = ((row % 128) // 4) * 16 + (row % 4) * 4 + row // 128
+    regroup = flag(jnp.broadcast_to(source, (512, 512)) == grid_index((512, 512), 1))
     blocks_c = nn(regroup.astype(BF), blocks_c).astype(BF)
     for c in range(4):
         share_out[c] = blocks_c[128 * c : 128 * c + 128]
-    share_in[t] = share_out[y]
-    for d in range(1, 8):
-        target = lax.rem(t + d, 8)
+    share_in[core * 4 + y] = share_out[y]
+    for d in range(1, 4):
+        owner = lax.rem(y + d, 4)
         sent.append(
-            send(share_out.at[target // 2], share_in.at[t], s_send.at[d - 1], s_recv.at[0], target, g)
-        )
+            send(
+                share_out.at[owner],
+                share_in.at[core * 4 + y],
+                s_send.at[d - 1],
+                s_recv.at[0],
+                owner * 2 + core,
+                g,
+            )
+        )
+
+    choose_b, half_b = [], []
+    lane384 = grid_index((8, 384), 1)
+    for n in range(4):
+        entry = column([v_lists_b[n : n + 1, :]], 24, 0) - (g - 1) * 32
+        valid = column([v_mask_b[n : n + 1, :]], 24, 0)
+        base = jnp.where(valid == 1, (entry // 2) * 8, -1000)
+        for i in range(3):
+            wide = jnp.broadcast_to(base[8 * i : 8 * i + 8], (8, 384)) - lane384
+            choose_b.extend(flag(wide == -r) for r in range(8))
+            half_b.append(jnp.broadcast_to(entry[8 * i : 8 * i + 8] % 2, (8, 128)) == lane // 64)
+    choose_b = jnp.concatenate(choose_b, axis=0).astype(BF)
+
+    pl.when(lower_half)(lambda: send_grand(here.at[0], half))
+    received(share_in.at[pl.ds(0, 3)], s_recv.at[0])
+    shares = share_in.at[pl.ds(core * 4, 4)]
+    sent.append(send(shares, shares, s_send.at[3], s_recv.at[1], mate, g))
+
+    for d in range(4):
+        source = core * 4 + lax.rem(y + 4 - d, 4)
+        for side in range(2):
+            block = leaf_window.at[source + 16 * side]
+            there = (has_down, has_up)[side]
+            received(block, x_recv.at[4 * side + d], there)
+            k = 4 + 2 * d + side
+            sent.append(send(block, block, mate_send.at[k], mate_recv.at[k], mate, g, there))
+
 
     row, col = grid_index((128, 256), 0), grid_index((128, 256), 1)
     same_p = row % 8 == col % 8
@@ -379,8 +405,10 @@
         ((row // 8) % 2 == col // 128) & (row % 8 == (col // 16) % 8) & (row // 16 == (col // 8) % 2)
     ).astype(BF)
     diagonal4 = row // 8 == col // 64
-    row, col = grid_index((512, 256), 0), grid_index((512, 256), 1)
-    expand = flag(col % 64 == 2 * ((row % 256) // 8) + row // 256).astype(BF)
+    row = grid_index((512, 1), 0)
+    target = 2 * ((row % 256) // 8) + row // 256
+    expand = flag(jnp.broadcast_to(target, (512, 128)) == grid_index((512, 128), 1) % 64).astype(BF)
+    expand = jnp.concatenate([expand, expand], axis=1)
     row, col = grid_index((32, 128), 0), grid_index((32, 128), 1)
     diagonal2 = (row // 8) % 2 == col // 64
     row, col = grid_index((16, 128), 0), grid_index((16, 128), 1)
@@ -415,6 +443,7 @@
             pair = []
     near_b = nn(jnp.concatenate(rows, axis=0), expand[:, 0:128])
 
+
     for k in range(4):
         if k == 0:
             block = leaf_window.at[8 + (1 - core) * 4 + y]
@@ -461,12 +490,26 @@
         folded[pl.ds(pl.multiple_of(16 * pair, 16), 16), :] = fold_pair(rows)
         return carry
 
-    lax.fori_loop(0, 32, build, 0, unroll=4)
-    lax.fori_loop(0, 32, multiply, 0, unroll=4)
-    lax.fori_loop(0, 16, fold_products, 0, unroll=4)
-    near[...] = nn(folded[...], expand)
-
-    received(share_in.at[pl.ds(0, 7)], s_recv.at[0])
+    lax.fori_loop(0, 32, build, 0, unroll=32)
+    lax.fori_loop(0, 32, multiply, 0, unroll=32)
+    lax.fori_loop(0, 16, fold_products, 0, unroll=16)
+    near_a = nn(folded[...], expand)
+    for h in range(2):
+        y_b = jnp.where(diagonal2[0:16], near_b[16 * h : 16 * h + 16], 0.0).astype(BF)
+        spread_b = nn(y_b, v_tb[128 * h : 128 * h + 128, :])
+        for j in range(2):
+            for k in range(2):
+                s = 4 * h + 2 * j + k
+                part = spread_b[8 * j : 8 * j + 8, 256 * k : 256 * k + 256]
+                near[32 * s : 32 * s + 32, :] = near_a[32 * s : 32 * s + 32] + jnp.concatenate([part] * 4, axis=0)
+
+    own_c = v_tc[pl.ds(pl.multiple_of(64 * y, 64), 64), :]
+    own_c = jnp.where(core == 0, own_c[:, 0:256].astype(F32), own_c[:, 256:512].astype(F32)).astype(BF)
+    down_c = jnp.concatenate(
+        [nn(own_c[:, 64 * b : 64 * b + 64], v_tb[64 * b : 64 * b + 64, :]) for b in range(4)], axis=1
+    ).astype(BF)
+
+    received(share_in.at[pl.ds(0, 4)], s_recv.at[1])
     grand_rows = 16 * groups
     row, lane32 = grid_index((32, 128), 0), grid_index((32, 128), 1)
     choose_c, half_c = [], []
@@ -500,23 +543,21 @@
     full = full[0:16] + full[16:32] + full[32:48] + full[48:64]
     y_c = nn(jnp.concatenate([full[0:8], full[8:16]], axis=1).astype(BF), expand_c).astype(BF)
 
-    spread_c = nn(y_c, v_tc[pl.ds(pl.multiple_of(64 * y, 64), 64), :])
-    own_down = jnp.where(core == 0, spread_c[:, 0:256], spread_c[:, 256:512])
-    for h in range(2):
-        part = own_down[:, 128 * h : 128 * h + 128]
-        part = near_b[16 * h : 16 * h + 16] + jnp.concatenate([part, part], axis=0)
-        y_b = jnp.where(diagonal2[0:16], part, 0.0).astype(BF)
-        spread_b = nn(y_b, v_tb[128 * h : 128 * h + 128, :])
-        for j in range(2):
-            for k in range(2):
-                s = 4 * h + 2 * j + k
-                part = spread_b[8 * j : 8 * j + 8, 256 * k : 256 * k + 256]
-                part = near[32 * s : 32 * s + 32, :] + jnp.concatenate([part] * 4, axis=0)
-                y_a = jnp.where(diagonal4, part, 0.0).astype(BF)
-                field[32 * s : 32 * s + 32, :] = nn(y_a, v_basis[256 * s : 256 * s + 256, :]).astype(BF)
+    from_c = nn(y_c, down_c)
+    writes = []
+    for s in range(8):
+        part = from_c[:, 256 * s : 256 * s + 256]
+        part = near[32 * s : 32 * s + 32, :] + jnp.concatenate([part] * 4, axis=0)
+        y_a = jnp.where(diagonal4, part, 0.0).astype(BF)
+        rows = pl.ds(32 * s, 32)
+        field[rows, :] = nn(y_a, v_basis[256 * s : 256 * s + 256, :]).astype(BF)
+        writes.append(pltpu.make_async_copy(field.at[rows], out.at[rows], out_sem.at[s]))
+        writes[-1].start()
 
     for copy, when in sent:
         pl.when(when)(copy.wait_send)
+    for write in writes:
+        write.wait()
 
 
 def tiles(coupling):
@@ -557,13 +598,12 @@
         mask_c.transpose(2, 0, 1),
     )
     far = pl.BlockSpec(memory_space=pltpu.HBM)
-    local = pl.BlockSpec(memory_space=pltpu.VMEM)
     dma = pltpu.SemaphoreType.DMA
     field = pl.pallas_call(
         functools.partial(kernel, groups),
         out_shape=jax.ShapeDtypeStruct((256, 256), BF),
         in_specs=[far] * 13,
-        out_specs=local,
+        out_specs=far,
         scratch_shapes=[pltpu.VMEM(x.shape, x.dtype) for x in operands]
         + [
             pltpu.VMEM((24, 128, 128), BF),
@@ -577,9 +617,11 @@
             pltpu.VMEM((32, 128, 256), BF),
             pltpu.VMEM((256, 512), BF),
             pltpu.VMEM((256, 256), F32),
+            pltpu.VMEM((256, 256), BF),
+            dma((8,)),
         ]
         + [dma((k,)) for k in (13, 3, 3, 8, 8, 12, 12, 7, 1, 2, 2, groups - 1, 1)]
-        + [pltpu.SemaphoreType.REGULAR((3,)), dma((7,)), dma((1,))],
+        + [pltpu.SemaphoreType.REGULAR((3,)), dma((4,)), dma((2,))],
         compiler_params=pltpu.CompilerParams(
             collective_id=0, has_side_effects=True, vmem_limit_bytes=60 * 1024 * 1024
         ),

time: 30.5 us -> 27.4 us (0.90)
  Pallas kernels: 28.6 us -> 25.5 us
    pallas_call x1, Pallas kernels: 28.6 us -> 25.5 us  [on_device(): pl.pallas_call(functools.partial(kernel, groups), out_shape=jax.ShapeDtyp...]
where the time goes in v3:
time: 27.4 us; the launch traced here: 27 us
  Pallas kernels  25.5 us (93%)
  local copies, waits for them, and re-layouts  1.57 us (6%)
    pallas_call x1, Pallas kernels, on_device(): pl.pallas_call(functools.partial(kernel, groups), out_shape=jax.ShapeDtyp...  25.5 us
    unnamed x1, local copies, waits for them, and re-layouts  1.57 us

profile of v3, /device:TPU:102, one launch (start us, length us, event | category | flops | bytes accessed | tf_op | source)
XLA Modules:
  0.0 27.0 jit_solution(12115220728567742275)
XLA Ops:
  0.0 25.5 %far_field.1 = bf16[256,256]{1,0:T(8,128)(2,1)} custom-call(bf16[256,256]{1,0:T(8,128)(2,1)} %bitcast.34, bf16[2048,256]{1,0:T(8,128)(2,1)} %bitcast.30, bf16[256,512]{1,0:T(8,128)(2,1)} %bitcast.32, bf16[256,512]{1,0:T(8,128)(2,1)} %bitcast.33, bf16[32,768,128]{2,1,0:T(8,128)(2,1)} %bitcast.29, bf16[4,768,128]{2,1,0:T(8,128)(2,1)} %bitcast.31, ...), custom_call_target="tpu_custom_call" | custom-call | flops 5000000000 | bytes 10000000 | tf_op jit(solution)/shard_map/far_field/pallas_call | solution.py:602
  25.5 1.6 %copy.15 = bf16[1,32,8,256]{3,2,1,0:T(8,128)(2,1)} copy(bf16[1,32,8,256]{3,2,1,0:T(8,128)(2,1)} %bitcast.28) | data formatting | bytes 262144

commit v4 on v3

--- a/solution.py
+++ b/solution.py
@@ -171,8 +171,11 @@
 
     signal_half(barrier, half, lower_half)
     signal_plane(0, (1, 2, 3), True)
-    signal_plane(1, range(4), (z < depth - 1) & (z != depth // 2 - 1))
-    signal_plane(-1, range(4), z > 0)
+    signal_plane(1, range(4), upper_half & (z < depth - 1))
+    signal_plane(-1, range(4), z > depth // 2)
+    first_x, last_x = g % 4 == 0, g % 4 == 3
+    pl.when(lower_half & last_x & (z < depth // 2 - 1))(lambda: signal(barrier, g + 1))
+    pl.when(first_x & (z > 0) & (z <= depth // 2))(lambda: signal(barrier, g - 1))
 
     sub, lane = grid_index((8, 128), 0), grid_index((8, 128), 1)
     left = lane < 64
@@ -186,9 +189,8 @@
             leaf_window[first : first + 8] = jnp.zeros((8, 128, 128), BF)
             parent_window[first : first + 8] = jnp.zeros((8, 16, 128), BF)
 
-    beside = (z > 0).astype(jnp.int32) + (z < depth - 1).astype(jnp.int32)
-    beside = beside - (z == depth // 2).astype(jnp.int32)
-    pl.semaphore_wait(barrier, 10 + 4 * beside + half * upper_half.astype(jnp.int32))
+    beside = (z > depth // 2).astype(jnp.int32) + (z < depth - 1).astype(jnp.int32)
+    pl.when(upper_half)(lambda: pl.semaphore_wait(barrier, 10 + 4 * beside + half))
     signal_half(here.at[0], 0, upper_half)
     pl.when(upper_half & (z < depth - 1))(lambda: signal(here.at[1], g + 4))
     pl.when(upper_half & (z > depth // 2))(lambda: signal(here.at[1], g - 4))
@@ -236,6 +238,9 @@
         )
         pl.when(when)(copy.start)
         return copy, when
+
+    ends = last_x.astype(jnp.int32) + (first_x & (z > 0)).astype(jnp.int32)
+    pl.when(lower_half)(lambda: pl.semaphore_wait(barrier, 10 + ends))
 
     sent = []
     for d in range(1, 8):
@@ -444,6 +449,32 @@
     near_b = nn(jnp.concatenate(rows, axis=0), expand[:, 0:128])
 
 
+    own_c = v_tc[pl.ds(pl.multiple_of(64 * y, 64), 64), :]
+    own_c = jnp.where(core == 0, own_c[:, 0:256].astype(F32), own_c[:, 256:512].astype(F32)).astype(BF)
+    down_c = jnp.concatenate(
+        [nn(own_c[:, 64 * b : 64 * b + 64], v_tb[64 * b : 64 * b + 64, :]) for b in range(4)], axis=1
+    ).astype(BF)
+
+    received(share_in.at[pl.ds(0, 4)], s_recv.at[1])
+    grand_rows = 16 * groups
+    row, lane32 = grid_index((32, 128), 0), grid_index((32, 128), 1)
+    choose_c, half_c = [], []
+    for source in range(8):
+        code = jnp.broadcast_to(share_in[source, 0:16, :].astype(F32)[3:4], (32, 128))
+        code = jnp.sum(jnp.where(lane32 == row // 8, code, 0.0), axis=1, keepdims=True).astype(jnp.int32)
+        row1 = grid_index((32, 1), 0)
+        base = jnp.where((code >= 0) & (row1 < 24), (code // 2) * 8 + row1 % 8, -1000)
+        hit = jnp.broadcast_to(base, (32, grand_rows)) == grid_index((32, grand_rows), 1)
+        choose_c.append(flag(hit))
+        half_c.append(jnp.broadcast_to(code % 2, (32, 128)) == lane32 // 64)
+    choose_c = jnp.concatenate(choose_c, axis=0).astype(BF)
+    half_c = jnp.concatenate(half_c, axis=0)
+    blocks_c = jnp.concatenate([share_in[source] for source in range(8)], axis=1)
+    row, col = grid_index((64, 128), 0), grid_index((64, 128), 1)
+    same_c = row // 16 == col % 4
+    row, col = grid_index((256, 64), 0), grid_index((256, 64), 1)
+    expand_c = flag(col == 2 * ((row % 128) // 4) + row // 128).astype(BF)
+
     for k in range(4):
         if k == 0:
             block = leaf_window.at[8 + (1 - core) * 4 + y]
@@ -502,32 +533,6 @@
                 s = 4 * h + 2 * j + k
                 part = spread_b[8 * j : 8 * j + 8, 256 * k : 256 * k + 256]
                 near[32 * s : 32 * s + 32, :] = near_a[32 * s : 32 * s + 32] + jnp.concatenate([part] * 4, axis=0)
-
-    own_c = v_tc[pl.ds(pl.multiple_of(64 * y, 64), 64), :]
-    own_c = jnp.where(core == 0, own_c[:, 0:256].astype(F32), own_c[:, 256:512].astype(F32)).astype(BF)
-    down_c = jnp.concatenate(
-        [nn(own_c[:, 64 * b : 64 * b + 64], v_tb[64 * b : 64 * b + 64, :]) for b in range(4)], axis=1
-    ).astype(BF)
-
-    received(share_in.at[pl.ds(0, 4)], s_recv.at[1])
-    grand_rows = 16 * groups
-    row, lane32 = grid_index((32, 128), 0), grid_index((32, 128), 1)
-    choose_c, half_c = [], []
-    for source in range(8):
-        code = jnp.broadcast_to(share_in[source, 0:16, :].astype(F32)[3:4], (32, 128))
-        code = jnp.sum(jnp.where(lane32 == row // 8, code, 0.0), axis=1, keepdims=True).astype(jnp.int32)
-        row1 = grid_index((32, 1), 0)
-        base = jnp.where((code >= 0) & (row1 < 24), (code // 2) * 8 + row1 % 8, -1000)
-        hit = jnp.broadcast_to(base, (32, grand_rows)) == grid_index((32, grand_rows), 1)
-        choose_c.append(flag(hit))
-        half_c.append(jnp.broadcast_to(code % 2, (32, 128)) == lane32 // 64)
-    choose_c = jnp.concatenate(choose_c, axis=0).astype(BF)
-    half_c = jnp.concatenate(half_c, axis=0)
-    blocks_c = jnp.concatenate([share_in[source] for source in range(8)], axis=1)
-    row, col = grid_index((64, 128), 0), grid_index((64, 128), 1)
-    same_c = row // 16 == col % 4
-    row, col = grid_index((256, 64), 0), grid_index((256, 64), 1)
-    expand_c = flag(col == 2 * ((row % 128) // 4) + row // 128).astype(BF)
 
     received(grand_window.at[pl.ds(0, groups - 1)], c_recv.at[0])
     found = nn(choose_c, grand_window[...].reshape(grand_rows, 128))

time: 27.4 us -> 27.1 us (0.989)
  no operation moved by 1% of the time
where the time goes in v4:
time: 27.1 us; the launch traced here: 27 us
  Pallas kernels  25.4 us (94%)
  local copies, waits for them, and re-layouts  1.57 us (6%)
    pallas_call x1, Pallas kernels, on_device(): pl.pallas_call(functools.partial(kernel, groups), out_shape=jax.ShapeDtyp...  25.4 us
    unnamed x1, local copies, waits for them, and re-layouts  1.57 us

profile of v4, /device:TPU:102, one launch (start us, length us, event | category | flops | bytes accessed | tf_op | source)
XLA Modules:
  0.0 27.0 jit_solution(4234685893458778514)
XLA Ops:
  0.0 25.4 %far_field.1 = bf16[256,256]{1,0:T(8,128)(2,1)} custom-call(bf16[256,256]{1,0:T(8,128)(2,1)} %bitcast.34, bf16[2048,256]{1,0:T(8,128)(2,1)} %bitcast.30, bf16[256,512]{1,0:T(8,128)(2,1)} %bitcast.32, bf16[256,512]{1,0:T(8,128)(2,1)} %bitcast.33, bf16[32,768,128]{2,1,0:T(8,128)(2,1)} %bitcast.29, bf16[4,768,128]{2,1,0:T(8,128)(2,1)} %bitcast.31, ...), custom_call_target="tpu_custom_call" | custom-call | flops 5000000000 | bytes 10000000 | tf_op jit(solution)/shard_map/far_field/pallas_call | solution.py:607
  25.4 1.6 %copy.15 = bf16[1,32,8,256]{3,2,1,0:T(8,128)(2,1)} copy(bf16[1,32,8,256]{3,2,1,0:T(8,128)(2,1)} %bitcast.28) | data formatting | bytes 262144

commit v5 on v4

--- a/solution.py
+++ b/solution.py
@@ -330,14 +330,6 @@
 
     pl.when(upper_half)(lambda: send_grand(here.at[2], 1))
 
-    group_parents = parent_window.at[pl.ds(8, 8)]
-    sent.append(
-        send(group_parents, parent_window.at[pl.ds(0, 8)], bx_send.at[0], bx_recv.at[0], t, up, has_up)
-    )
-    sent.append(
-        send(group_parents, parent_window.at[pl.ds(16, 8)], bx_send.at[1], bx_recv.at[1], t, down, has_down)
-    )
-
     loads[4].wait()
     for load in loads[9:13]:
         load.wait()
@@ -388,7 +380,16 @@
             half_b.append(jnp.broadcast_to(entry[8 * i : 8 * i + 8] % 2, (8, 128)) == lane // 64)
     choose_b = jnp.concatenate(choose_b, axis=0).astype(BF)
 
-    pl.when(lower_half)(lambda: send_grand(here.at[0], half))
+    group_parents = parent_window.at[pl.ds(8, 8)]
+    sent.append(
+        send(group_parents, parent_window.at[pl.ds(0, 8)], bx_send.at[0], bx_recv.at[0], t, up, has_up)
+    )
+    sent.append(
+        send(group_parents, parent_window.at[pl.ds(16, 8)], bx_send.at[1], bx_recv.at[1], t, down, has_down)
+    )
+
+    late = lower_half & last_x & (z == depth // 2 - 1)
+    pl.when(late)(lambda: send_grand(here.at[0], half))
     received(share_in.at[pl.ds(0, 3)], s_recv.at[0])
     shares = share_in.at[pl.ds(core * 4, 4)]
     sent.append(send(shares, shares, s_send.at[3], s_recv.at[1], mate, g))
@@ -426,6 +427,8 @@
     def fold_pair(pair):
         both = nn(fold, pair)
         return jnp.concatenate([both[0:16], both[16:32]], axis=1).astype(BF)
+
+    pl.when(lower_half & jnp.logical_not(late))(lambda: send_grand(here.at[0], half))
 
     received(parent_window.at[pl.ds(0, 8)], bx_recv.at[0], has_down)
     received(parent_window.at[pl.ds(16, 8)], bx_recv.at[1], has_up)

time: 27.1 us -> 27 us (level)
  no operation moved by 1% of the time
where the time goes in v5:
time: 27 us; the launch traced here: 26.9 us
  Pallas kernels  25.4 us (94%)
  local copies, waits for them, and re-layouts  1.57 us (6%)
    pallas_call x1, Pallas kernels, on_device(): pl.pallas_call(functools.partial(kernel, groups), out_shape=jax.ShapeDtyp...  25.4 us
    unnamed x1, local copies, waits for them, and re-layouts  1.57 us

profile of v5, /device:TPU:102, one launch (start us, length us, event | category | flops | bytes accessed | tf_op | source)
XLA Modules:
  0.0 26.9 jit_solution(17877619595294175746)
XLA Ops:
  0.0 25.4 %far_field.1 = bf16[256,256]{1,0:T(8,128)(2,1)} custom-call(bf16[256,256]{1,0:T(8,128)(2,1)} %bitcast.34, bf16[2048,256]{1,0:T(8,128)(2,1)} %bitcast.30, bf16[256,512]{1,0:T(8,128)(2,1)} %bitcast.32, bf16[256,512]{1,0:T(8,128)(2,1)} %bitcast.33, bf16[32,768,128]{2,1,0:T(8,128)(2,1)} %bitcast.29, bf16[4,768,128]{2,1,0:T(8,128)(2,1)} %bitcast.31, ...), custom_call_target="tpu_custom_call" | custom-call | flops 5000000000 | bytes 10000000 | tf_op jit(solution)/shard_map/far_field/pallas_call | solution.py:610
  25.4 1.6 %copy.15 = bf16[1,32,8,256]{3,2,1,0:T(8,128)(2,1)} copy(bf16[1,32,8,256]{3,2,1,0:T(8,128)(2,1)} %bitcast.28) | data formatting | bytes 262144
